TPU v7x, 512 devices: a whole 4x8x8 slice. The times are simulated.
512 devices in a mesh: slab: 8 (over x, core), coil: 16 (over z_lo, y), row: 4 (over z_hi).
Axes of the slice: x: 4, y: 8, z: 8 (z_hi: 4, z_lo: 2; z = z_hi * 2 + z_lo), core: 2. Of those that a mesh axis runs over, the one named last changes fastest.
Arguments:
- solution: float32 [2, 8, 384, 384], P(None, 'slab', 'row'), may hold values from -6 to 6
- residual: float32 [2, 8, 384, 384], P(None, 'slab', 'row'), may hold values from -90 to 90
- direction: float32 [2, 8, 384, 384], P(None, 'slab', 'row'), may hold values from -90 to 90
- sens: bfloat16 [2, 32, 8, 384, 384], P(None, 'coil', 'slab', 'row'), may hold values from -0.75 to 0.75
- sample_cell: int32 [2048], P('row'), may hold values from 0 to 36863
- kernel: float32 [2, 5, 2048], P(None, None, 'row'), may hold values from 0.2 to 1
- density: float32 [2048], P('row'), may hold values from 0.5 to 4
Outputs:
- solution_next: float32 [2, 8, 384, 384], P(None, 'slab', 'row')
- residual_next: float32 [2, 8, 384, 384], P(None, 'slab', 'row')
- direction_next: float32 [2, 8, 384, 384], P(None, 'slab', 'row')
All inputs are finite; a program needn't handle non-finite values.
Results may differ from a plain program's by a relative error of at most 0.0003.
Values sent between devices are 32-bit elements; how exact they have to be, the bound alone decides.
A program may use at most 64 MiB of HBM per device.

v0:
```python
import math

import jax
import jax.numpy as jnp
from jax import lax
from jax.sharding import PartitionSpec as P

damping = 0.05
highest = lax.Precision.HIGHEST


def padded(block, sides, width):
    for axis, dim in sides:
        count = lax.axis_size(axis)
        forward = [(i, i + 1) for i in range(count - 1)]
        forward.append((count - 1, 0))
        backward = [(target, source) for source, target in forward]
        low = lax.ppermute(
            lax.slice_in_dim(block, block.shape[dim] - width, None, axis=dim), axis, forward
        )
        high = lax.ppermute(lax.slice_in_dim(block, 0, width, axis=dim), axis, backward)
        block = jnp.concatenate([low, block, high], axis=dim)
    return block


def partner_2(block, axis, distance):
    count = lax.axis_size(axis)
    route = []
    for low in range(count):
        high = low | 1 << distance
        if high != low and high < count:
            route += [(low, high), (high, low)]
    return lax.ppermute(block, axis, route)


def dft_tables(length):
    positions = jnp.arange(length, dtype=jnp.int32)
    phase_index = positions[:, None] * positions[None, :] % length
    angles = phase_index.astype(jnp.float32) * (2.0 * math.pi / length)
    scaling = 1.0 / math.sqrt(length)
    return (jnp.cos(angles) * scaling, jnp.sin(angles) * scaling)


def complex_product(real_part, imag_part, cosine, sine, orientation, pattern):

    def product(operand, table):
        return jnp.einsum(pattern, operand, table, precision=highest)

    real_out = product(real_part, cosine) - orientation * product(imag_part, sine)
    imag_out = product(imag_part, cosine) + orientation * product(real_part, sine)
    return (real_out, imag_out)


def column_rims(grid_part):
    return padded(grid_part, (("row", 2),), 2)


def norm_sum(field):
    return lax.psum(jnp.sum(field * field), ("slab", "row"))


def on_device(solution, residual, direction, sens, sample_cell, kernel, density):
    length = direction.shape[3]
    band_count = lax.axis_size("row")
    band_cols = length // band_count
    cosine, sine = dft_tables(length)
    half_bit = lax.axis_size("slab").bit_length() - 2
    sens_real = sens[0].astype(jnp.float32)
    sens_imag = sens[1].astype(jnp.float32)
    coil_real = sens_real * direction[0][None] - sens_imag * direction[1][None]
    coil_imag = sens_real * direction[1][None] + sens_imag * direction[0][None]
    paired = jnp.stack([coil_real, coil_imag])
    partner = partner_2(paired, "slab", half_bit)
    paired = 0.5 * (paired + partner)
    coil_real, coil_imag = (paired[0], paired[1])
    k_real, k_imag = complex_product(coil_real, coil_imag, cosine, sine, -1.0, "cdrn,nk->cdrk")
    coil_count, slice_count, row_count = (k_real.shape[0], k_real.shape[1], k_real.shape[2])
    stacked = jnp.stack([k_real, k_imag]).reshape(2, coil_count * slice_count, row_count, length)
    tap_count = kernel.shape[1]
    half_taps = tap_count // 2
    sample_col = sample_cell // length
    sample_row = sample_cell % length
    row_cells = jnp.arange(length, dtype=jnp.int32)[:, None]
    col_cells = jnp.arange(band_cols + 4, dtype=jnp.int32)[:, None]
    row_weight = jnp.zeros((length, sample_cell.shape[0]), jnp.float32)
    col_weight = jnp.zeros((band_cols + 4, sample_cell.shape[0]), jnp.float32)
    for tap in range(tap_count):
        row_target = (sample_row + tap - half_taps) % length
        row_weight = row_weight + jnp.where(
            row_cells == row_target[None], kernel[0, tap][None], 0.0
        )
        col_weight = col_weight + jnp.where(
            col_cells == (sample_col + tap)[None], kernel[1, tap][None], 0.0
        )
    pieces = lax.all_to_all(stacked, "row", split_axis=3, concat_axis=2, tiled=True)
    item_count = pieces.shape[1]
    g_real, g_imag = complex_product(pieces[0], pieces[1], cosine, sine, -1.0, "bnw,nk->bwk")
    grid_cells = jnp.stack([g_real, g_imag])
    extended = column_rims(grid_cells)
    flattened = extended.reshape(2 * item_count, band_cols + 4, length)
    along_rows = jnp.einsum("bck,ks->bcs", flattened, row_weight, precision=highest)
    values = jnp.sum(along_rows * col_weight[None], axis=1)
    values = values * density[None]
    weighted_cols = values[:, None, :] * col_weight[None]
    spread = jnp.einsum("bcs,ks->bck", weighted_cols, row_weight, precision=highest)
    spread = spread.reshape(2, item_count, band_cols + 4, length)
    border_cols = jnp.concatenate([spread[:, :, :2], spread[:, :, band_cols + 2 :]], axis=2)
    received = column_rims(border_cols)
    interior = spread[:, :, 2 : band_cols + 2]
    interior = interior.at[:, :, :2].add(received[:, :, :2])
    interior = interior.at[:, :, band_cols - 2 :].add(received[:, :, 6:])
    i_real, i_imag = complex_product(interior[0], interior[1], cosine, sine, 1.0, "bwk,kn->bnw")
    image_cols = jnp.stack([i_real, i_imag])
    returned = lax.all_to_all(image_cols, "row", split_axis=2, concat_axis=3, tiled=True)
    returned = returned.reshape(2, coil_count, slice_count, row_count, length)
    b_real, b_imag = complex_product(returned[0], returned[1], cosine, sine, 1.0, "cdrk,kn->cdrn")
    term_real = jnp.sum(sens_real * b_real + sens_imag * b_imag, axis=0)
    term_imag = jnp.sum(sens_real * b_imag - sens_imag * b_real, axis=0)
    coil_sum = lax.psum(jnp.stack([term_real, term_imag]), "coil")
    normal_image = coil_sum + damping * direction
    norm_now = norm_sum(residual)
    curvature = lax.psum(jnp.sum(direction * normal_image), ("slab", "row"))
    step_length = norm_now / curvature
    solution_next = solution + step_length * direction
    residual_next = residual - step_length * normal_image
    norm_next = norm_sum(residual_next)
    direction_next = residual_next + norm_next / norm_now * direction
    return (solution_next, residual_next, direction_next)


def solution(mesh):
    return jax.shard_map(
        on_device,
        mesh=mesh,
        in_specs=(
            P(None, "slab", "row", None),
            P(None, "slab", "row", None),
            P(None, "slab", "row", None),
            P(None, "coil", "slab", "row", None),
            P("row"),
            P(None, None, "row"),
            P("row"),
        ),
        out_specs=(
            P(None, "slab", "row", None),
            P(None, "slab", "row", None),
            P(None, "slab", "row", None),
        ),
        check_vma=False,
    )
```

profile of v0, /device:TPU:16, one launch (start us, length us, event | category | flops | bytes accessed | tf_op | source)
XLA Modules:
  0.0 457.9 jit_solution(2023091795412439456)
XLA Ops:
  8.4 4.9 %collective-permute-start = (f32[2,2,1,96,384]{4,3,1,2,0:T(8,128)S(1)}, f32[2,2,1,96,384]{4,3,1,2,0:T(8,128)S(1)}, u32[]{:S(2)}, u32[]{:S(2)}) collective-permute-start(f32[2,2,1,96,384]{4,3,1,2,0:T(8,128)S(1)} %pad_maximum_fusion.1), channel_id=1, source_target_pairs={{0,256},{256,0},{64,320},{320,64},{128,384},{384,128},{192,448},{4... | collective-permute-start | bytes 1769480 | tf_op jit(solution)/shard_map/ppermute | solution.py:33
  13.3 13.5 %collective-permute-done = f32[2,2,1,96,384]{4,3,1,2,0:T(8,128)S(1)} collective-permute-done((f32[2,2,1,96,384]{4,3,1,2,0:T(8,128)S(1)}, f32[2,2,1,96,384]{4,3,1,2,0:T(8,128)S(1)}, u32[]{:S(2)}, u32[]{:S(2)}) %collective-permute-start) | collective-permute-done | bytes 589856 | tf_op jit(solution)/shard_map/ppermute | solution.py:33
  26.9 3.0 convolution_multiply_fusion.4
  30.0 3.0 convolution_multiply_fusion.3
  36.0 3.3 fusion.5
  40.5 10.4 %all-to-all-start = ((f32[2,2,96,384]{2,1,0,3:T(2,128)}), f32[2,2,96,384]{2,1,0,3:T(2,128)S(1)}, u32[]{:S(2)}, u32[]{:S(2)}) async-start(f32[2,2,96,384]{2,1,0,3:T(2,128)} %copy.18), calls=%async_computation | async-start | bytes 1572864 | tf_op jit(solution)/shard_map/all_to_all | solution.py:95
  51.7 16.0 %all-to-all-done = f32[2,2,96,384]{2,1,0,3:T(2,128)S(1)} async-done(((f32[2,2,96,384]{2,1,0,3:T(2,128)}), f32[2,2,96,384]{2,1,0,3:T(2,128)S(1)}, u32[]{:S(2)}, u32[]{:S(2)}) %all-to-all-start) | async-done | bytes 589856 | tf_op jit(solution)/shard_map/all_to_all | solution.py:95
  68.5 3.0 convolution_multiply_fusion.2
  71.8 3.0 convolution_multiply_fusion.1
  74.8 3.0 fusion.4
  80.8 7.0 %collective-permute-start.1 = (f32[2,2,2,384]{3,2,1,0:T(2,128)S(1)}, f32[2,2,2,384]{3,2,1,0:T(2,128)S(1)}, u32[]{:S(2)}, u32[]{:S(2)}) collective-permute-start(f32[2,2,2,384]{3,2,1,0:T(2,128)S(1)} %get-tuple-element.41), channel_id=1, source_target_pairs={{0,1},{1,2},{2,3},{3,0},{4,5},{5,6},{6,7},{7,4},{8,9},{9,10},{10,1... | collective-permute-start | bytes 36872 | tf_op jit(solution)/shard_map/ppermute | solution.py:18
  90.8 3.6 collective-permute-done.2
  98.6 3.7 collective-permute-start.3
  102.3 13.7 %collective-permute-start.4 = (f32[2,2,2,384]{3,2,1,0:T(2,128)S(1)}, f32[2,2,2,384]{3,2,1,0:T(2,128)S(1)}, u32[]{:S(2)}, u32[]{:S(2)}) collective-permute-start(f32[2,2,2,384]{3,2,1,0:T(2,128)S(1)} %get-tuple-element.39), channel_id=1, source_target_pairs={{1,0},{2,1},{3,2},{0,3},{5,4},{6,5},{7,6},{4,7},{9,8},{10,9},{11,1... | collective-permute-start | bytes 36872 | tf_op jit(solution)/shard_map/ppermute | solution.py:21
  116.1 3.0 fusion.17
  119.1 3.0 fusion.15
  122.1 3.0 fusion.2
  125.2 3.0 fusion.1
  128.9 20.5 %all_to_all.30 = f32[2,2,384,96]{3,1,0,2:T(2,128)S(1)} all-to-all(f32[2,2,384,96]{3,1,0,2:T(2,128)S(1)} %copy.20), channel_id=1, replica_groups=mesh['slab'=8,'coil'=16,'row'=4] {'row'}, dimensions={2} | all-to-all | bytes 1179648 | tf_op jit(solution)/shard_map/all_to_all | solution.py:114
  156.4 3.0 convolution_add_fusion
  159.4 3.7 fusion.65
  165.5 134.1 %all-reduce.3.cloned.1.call-done = f32[2,1,96,384]{3,2,1,0:T(8,128)} async-done(((f32[2,1,96,384]{3,2,1,0:T(8,128)}), f32[2,1,96,384]{3,2,1,0:T(8,128)}) %all-reduce.3.cloned.1.call-update) | async-done | bytes 294928 | tf_op jit(solution)/shard_map/psum | solution.py:119
  301.3 73.2 %all-reduce = (f32[]{:T(128)}, f32[]{:T(128)}) all-reduce(f32[]{:T(128)} %multiply_reduce_fusion.2, f32[]{:T(128)} %multiply_reduce_fusion.1), channel_id=1, replica_groups=mesh['slab'=8,'coil'=16,'row'=4] {'slab','row'}, use_global_device_ids=true, to_apply=%region_1.2 | all-reduce | flops 2 | bytes 16 | tf_op jit(solution)/shard_map/psum | solution.py:59
  376.5 72.0 %psum.31 = f32[]{:T(128)} all-reduce(f32[]{:T(128)} %get-tuple-element.31), channel_id=1, replica_groups=mesh['slab'=8,'coil'=16,'row'=4] {'slab','row'}, use_global_device_ids=true, to_apply=%region_9.10 | all-reduce | flops 1 | bytes 8 | tf_op jit(solution)/shard_map/psum | solution.py:59
  (62 shorter events, 30.7 us)
Async XLA Ops:
  7.2 1.1 copy-start.5
  8.4 18.5 %collective-permute-start = (f32[2,2,1,96,384]{4,3,1,2,0:T(8,128)S(1)}, f32[2,2,1,96,384]{4,3,1,2,0:T(8,128)S(1)}, u32[]{:S(2)}, u32[]{:S(2)}) collective-permute-start(f32[2,2,1,96,384]{4,3,1,2,0:T(8,128)S(1)} %pad_maximum_fusion.1), channel_id=1, source_target_pairs={{0,256},{256,0},{64,320},{320,64},{128,384},{384,128},{192,448},{4... | collective-permute-start | bytes 1769480 | tf_op jit(solution)/shard_map/ppermute | solution.py:33
  40.5 10.4 %copy-start.8 = (s32[512]{0:T(512)S(1)}, s32[512]{0:T(512)}, u32[]{:S(2)}) copy-start(s32[512]{0:T(512)} %param.15) | copy-start | bytes 6148
  40.5 27.2 %all-to-all-start = ((f32[2,2,96,384]{2,1,0,3:T(2,128)}), f32[2,2,96,384]{2,1,0,3:T(2,128)S(1)}, u32[]{:S(2)}, u32[]{:S(2)}) async-start(f32[2,2,96,384]{2,1,0,3:T(2,128)} %copy.18), calls=%async_computation | async-start | bytes 1572864 | tf_op jit(solution)/shard_map/all_to_all | solution.py:95
  50.9 0.7 copy-start.6
  51.0 248.6 %all-reduce.3.cloned.1.call-start = ((), (), s32[]{:S(2)}) async-start(), calls=%async_computation.2 | async-start | bytes 589824 | tf_op jit(solution)/shard_map/psum | solution.py:119
  80.8 10.0 %collective-permute-start.1 = (f32[2,2,2,384]{3,2,1,0:T(2,128)S(1)}, f32[2,2,2,384]{3,2,1,0:T(2,128)S(1)}, u32[]{:S(2)}, u32[]{:S(2)}) collective-permute-start(f32[2,2,2,384]{3,2,1,0:T(2,128)S(1)} %get-tuple-element.41), channel_id=1, source_target_pairs={{0,1},{1,2},{2,3},{3,0},{4,5},{5,6},{6,7},{7,4},{8,9},{9,10},{10,1... | collective-permute-start | bytes 36872 | tf_op jit(solution)/shard_map/ppermute | solution.py:18
  87.8 6.6 %collective-permute-start.2 = (f32[2,2,2,384]{3,2,1,0:T(2,128)S(1)}, f32[2,2,2,384]{3,2,1,0:T(2,128)S(1)}, u32[]{:S(2)}, u32[]{:S(2)}) collective-permute-start(f32[2,2,2,384]{3,2,1,0:T(2,128)S(1)} %get-tuple-element.42), channel_id=1, source_target_pairs={{1,0},{2,1},{3,2},{0,3},{5,4},{6,5},{7,6},{4,7},{9,8},{10,9},{11,1... | collective-permute-start | bytes 36872 | tf_op jit(solution)/shard_map/ppermute | solution.py:21
  94.4 2.1 copy-start.7
  98.6 17.4 %collective-permute-start.3 = (f32[2,2,2,384]{3,2,1,0:T(2,128)S(1)}, f32[2,2,2,384]{3,2,1,0:T(2,128)S(1)}, u32[]{:S(2)}, u32[]{:S(2)}) collective-permute-start(f32[2,2,2,384]{3,2,1,0:T(2,128)S(1)} %get-tuple-element.40), channel_id=1, source_target_pairs={{0,1},{1,2},{2,3},{3,0},{4,5},{5,6},{6,7},{7,4},{8,9},{9,10},{10,1... | collective-permute-start | bytes 36872 | tf_op jit(solution)/shard_map/ppermute | solution.py:18
  102.3 13.7 %collective-permute-start.4 = (f32[2,2,2,384]{3,2,1,0:T(2,128)S(1)}, f32[2,2,2,384]{3,2,1,0:T(2,128)S(1)}, u32[]{:S(2)}, u32[]{:S(2)}) collective-permute-start(f32[2,2,2,384]{3,2,1,0:T(2,128)S(1)} %get-tuple-element.39), channel_id=1, source_target_pairs={{1,0},{2,1},{3,2},{0,3},{5,4},{6,5},{7,6},{4,7},{9,8},{10,9},{11,1... | collective-permute-start | bytes 36872 | tf_op jit(solution)/shard_map/ppermute | solution.py:21
  163.8 1.0 copy-start.2
  163.8 135.7 %copy-start = (f32[2,1,96,384]{3,2,1,0:T(8,128)S(1)}, f32[2,1,96,384]{3,2,1,0:T(8,128)}, u32[]{:S(2)}) copy-start(f32[2,1,96,384]{3,2,1,0:T(8,128)} %param.13) | copy-start | bytes 884740
  299.6 76.3 %copy-start.3 = (f32[2,1,96,384]{3,2,1,0:T(8,128)S(1)}, f32[2,1,96,384]{3,2,1,0:T(8,128)}, u32[]{:S(2)}) copy-start(f32[2,1,96,384]{3,2,1,0:T(8,128)} %all-reduce.3.cloned.1.call-done) | copy-start | bytes 884740
  375.8 74.0 %copy-start.4 = (f32[2,1,96,384]{3,2,1,0:T(8,128)S(1)}, f32[2,1,96,384]{3,2,1,0:T(8,128)}, u32[]{:S(2)}) copy-start(f32[2,1,96,384]{3,2,1,0:T(8,128)} %param.11) | copy-start | bytes 884740
  376.5 74.2 %copy-start.1 = (f32[2,1,96,384]{3,2,1,0:T(8,128)}, f32[2,1,96,384]{3,2,1,0:T(8,128)S(1)}, u32[]{:S(2)}) copy-start(f32[2,1,96,384]{3,2,1,0:T(8,128)S(1)} %get-tuple-element.32) | copy-start | bytes 884740
Sparse Core Ops, SparseCore 0:
  164.0 135.5 all-reduce.2
where the time goes:
time: 467 us; the launch traced here: 458 us
  waiting for transfers between devices  167 us (36%)
  blocking collectives  166 us (36%)
  matrix products  53.1 us (11%)
  starting transfers between devices  42.5 us (9%)
  between operations  17.5 us (4%)
  local copies, waits for them, and re-layouts  6.62 us (1%)
  other arithmetic  5.19 us (1%)
    psum x2, blocking collectives, norm_sum(): return lax.psum(jnp.sum(field * field), ('slab', 'row'))  145 us
    psum x1, waiting for transfers between devices, on_device(): coil_sum = lax.psum(jnp.stack([term_real, term_imag]), 'coil')  134 us
    dot_general x16, matrix products, product(): return jnp.einsum(pattern, operand, table, precision=highest)  49 us
    all_to_all x1, blocking collectives, on_device(): lax.all_to_all(image_cols, 'row', split_axis=2, concat_axis=3, tiled=True)  20.5 us
    ppermute x2, starting transfers between devices, padded(): lax.ppermute(lax.slice_in_dim(block, 0, width, axis=dim), axis, backward)  16.5 us
    all_to_all x1, waiting for transfers between devices, on_device(): lax.all_to_all(stacked, 'row', split_axis=3, concat_axis=2, tiled=True)  16 us
    ppermute x1, waiting for transfers between devices, partner_2(): return lax.ppermute(block, axis, route)  13.5 us
    ppermute x2, starting transfers between devices, padded(): lax.ppermute(lax.slice_in_dim(block, block.shape[dim] - width, None, axis...  10.7 us
  transfers between devices with their start and end apart: 7, of which 4 were waited for; matrix products, arithmetic and copies ran while one was open for 0% of the time, Pallas kernels for 0%

commit v1 on v0

v1 whole, which is shorter than its diff:
```python
import functools
import math

import jax
import jax.numpy as jnp
import ml_dtypes
import numpy as np
from jax import lax
from jax.experimental import pallas as pl
from jax.experimental.pallas import tpu as pltpu
from jax.sharding import PartitionSpec as P

damping = 0.05
NXY = 384
BAND = 96
EXT = 128
HALO = 2
SAMP = 512
TAPS = 5
BLOCKS = 3
F32 = jnp.float32
BF16 = jnp.bfloat16
MESH = pl.DeviceIdType.MESH


def split_table(table):
    high = table.astype(np.float32).astype(ml_dtypes.bfloat16)
    low = (table - high.astype(np.float64)).astype(np.float32).astype(ml_dtypes.bfloat16)
    return high, low


def transform_tables(bands):
    x = np.arange(NXY)
    forward = np.zeros((bands, 2 * NXY, 2 * EXT))
    inverse = np.zeros((BLOCKS, bands * 2 * EXT, 256))
    scale = 1.0 / math.sqrt(NXY)
    for band in range(bands):
        k = (band * BAND - HALO + np.arange(EXT)) % NXY
        angle = (x[:, None] * k[None, :] % NXY) * (2.0 * math.pi / NXY)
        cosine, sine = np.cos(angle) * scale, np.sin(angle) * scale
        forward[band] = np.block([[cosine, -sine], [sine, cosine]])
        back = np.block([[cosine.T, sine.T], [-sine.T, cosine.T]])
        rows = slice(band * 2 * EXT, (band + 1) * 2 * EXT)
        for block in range(BLOCKS):
            cols = slice(block * 128, (block + 1) * 128)
            inverse[block, rows, :128] = back[:, :NXY][:, cols]
            inverse[block, rows, 128:] = back[:, NXY:][:, cols]
    return split_table(forward) + split_table(inverse)


def halves(value):
    high = value.astype(BF16)
    return high, (value - high.astype(F32)).astype(BF16)


def fold_phase(index):
    turn = index - NXY * jnp.floor(index * (1.0 / NXY) + 0.5)
    size = jnp.abs(turn)

    def sine_quarter(u):
        t = u * (2.0 * math.pi / NXY)
        q = t * t
        p = 1.0 / 6227020800.0
        for c in (-1.0 / 39916800.0, 1.0 / 362880.0, -1.0 / 5040.0, 1.0 / 120.0, -1.0 / 6.0, 1.0):
            p = p * q + c
        return p * t

    quarter = NXY // 4
    cosine = sine_quarter(quarter - size)
    sine = sine_quarter(quarter - jnp.abs(size - quarter))
    return cosine, jnp.where(turn < 0.0, -sine, sine)


def dot(a, b):
    return lax.dot_general(a, b, (((1,), (0,)), ((), ())), preferred_element_type=F32)


def dot_nt(a, b):
    return lax.dot_general(a, b, (((1,), (1,)), ((), ())), preferred_element_type=F32)


def kernel(
    rows_n, groups_n, ys_n,
    dir_ref, res_ref, sens_ref, cell_ref, kern_ref, dens_ref,
    fh_ref, fl_ref, bh_ref, bl_ref,
    n_ref, scal_ref,
    lhs_h, lhs_l, ke_h, ke_l, sinfo, cw, wr, tbuf, yconst, a_h, a_l, s_h, s_l,
    vsend, vrecv, wall, tz, zrecv, yrecv, ysum, nbuf, rz,
    g1, z1, y1, e2, g2, z2, y2,
    info_s, info_r, val_s, val_r, wt_s, wt_r,
    g1_s, g1_r, z1_s, z1_r, y1_s, y1_r,
    e2_s, e2_r, g2_s, g2_r, z2_s, z2_r, y2_s, y2_r,
    zr_s, zr_r, yr_s, yr_r, ya_s, ya_r, za_s, za_r,
):
    slab = lax.axis_index("slab")
    coil = lax.axis_index("coil")
    row = lax.axis_index("row")
    pair = slab // groups_n
    group = slab % groups_n
    zl = coil // ys_n
    yy = coil % ys_n
    half = SAMP // 128

    def remote(src, dst, send, recv, slab_to=None, coil_to=None, row_to=None):
        target = (
            slab if slab_to is None else slab_to,
            coil if coil_to is None else coil_to,
            row if row_to is None else row_to,
        )
        copy = pltpu.make_async_remote_copy(
            src_ref=src, dst_ref=dst, send_sem=send, recv_sem=recv,
            device_id=target, device_id_type=MESH,
        )
        copy.start()
        started.append(copy)
        return copy

    started = []

    eight = [(k, e) for k in range(rows_n) for e in range(2) if (k, e) != (0, 0)]

    def eight_to(k, e):
        return (group + groups_n * ((pair + e) % 2), (row + k) % rows_n)

    barrier = pltpu.get_barrier_semaphore()
    count = 0
    for k, e in eight:
        s, r = eight_to(k, e)
        pl.semaphore_signal(barrier, inc=1, device_id=(s, coil, r), device_id_type=MESH)
        count += 1
    for k in range(1, groups_n):
        s = (group + k) % groups_n + groups_n * pair
        pl.semaphore_signal(barrier, inc=1, device_id=(s, coil, row), device_id_type=MESH)
        count += 1
    pl.semaphore_signal(
        barrier, inc=1, device_id=(slab, (1 - zl) * ys_n + yy, row), device_id_type=MESH
    )
    count += 1
    for k in range(1, ys_n):
        c = zl * ys_n + (yy + k) % ys_n
        pl.semaphore_signal(barrier, inc=1, device_id=(slab, c, row), device_id_type=MESH)
        count += 1

    cell = cell_ref[...].astype(F32)
    kx = jnp.floor((cell + 0.5) * (1.0 / NXY))
    sinfo[row, 0:5, :] = kern_ref[0]
    sinfo[row, 5:10, :] = kern_ref[1]
    sinfo[row, 10:11, :] = cell - NXY * kx
    sinfo[row, 11:12, :] = kx

    pl.semaphore_wait(barrier, count)
    info = [None] + [
        remote(sinfo.at[row], sinfo.at[row], info_s.at[k], info_r.at[k], row_to=(row + k) % rows_n)
        for k in range(1, rows_n)
    ]

    for c in range(2):
        sr, si = sens_ref[0, c].astype(F32), sens_ref[1, c].astype(F32)
        dr, di = dir_ref[0], dir_ref[1]
        re_h, re_l = halves(sr * dr - si * di)
        im_h, im_l = halves(sr * di + si * dr)
        here = slice(c * BAND, (c + 1) * BAND)
        lhs_h[here, 0:NXY] = re_h
        lhs_h[here, NXY:] = im_h
        lhs_l[here, 0:NXY] = re_l
        lhs_l[here, NXY:] = im_l

    for band in range(rows_n):
        out = dot(lhs_h[...], fh_ref[band])
        out = out + dot(lhs_l[...], fh_ref[band])
        out = out + dot(lhs_h[...], fl_ref[band])
        high, low = halves(out)
        ke_h[band, 0:192] = high[:, :EXT]
        ke_h[band, 192:384] = high[:, EXT:]
        ke_l[band, 0:192] = low[:, :EXT]
        ke_l[band, 192:384] = low[:, EXT:]

    first = (row * BAND).astype(F32)
    ypos = lax.broadcasted_iota(jnp.int32, (BAND, 128), 0).astype(F32) + first
    c1, s1 = fold_phase(ypos)
    yconst[0] = c1
    yconst[1] = s1
    yconst[2] = 2.0 * c1 * c1 - 1.0
    yconst[3] = 2.0 * s1 * c1

    for b in range(BLOCKS):
        for plane in range(2):
            for g in range(24):
                rz[b, plane, g] = res_ref[plane, 4 * g : 4 * g + 4, 128 * b : 128 * (b + 1)]

    def wide(tile):
        return jnp.concatenate([tile] * half, axis=1)

    vals = {}
    for k in range(rows_n):
        band = (row + k) % rows_n
        if k:
            info[rows_n - k].wait_recv()
        ky = sinfo[band, 10:11, :]
        kxs = sinfo[band, 11:12, :]
        k0 = [sinfo[band, t : t + 1, :] for t in range(TAPS)]
        k1 = [sinfo[band, 5 + t : 6 + t, :] for t in range(TAPS)]
        cells = lax.broadcasted_iota(jnp.int32, (16, SAMP), 0).astype(F32)
        for g in range(8):
            if g < 7:
                offset = cells + (16.0 * g) - kxs
                weight = jnp.where(offset == 4.0, k1[4], 0.0)
                for t in range(3, -1, -1):
                    weight = jnp.where(offset == float(t), k1[t], weight)
                high, low = halves(weight)
            else:
                high = low = jnp.zeros((16, SAMP), BF16)
            cw[k, 16 * g : 16 * g + 16] = high
            cw[k, EXT + 16 * g : EXT + 16 * g + 16] = low
        low_pos = lax.broadcasted_iota(jnp.int32, (8, SAMP), 0).astype(F32)
        lo_c, lo_s = fold_phase(low_pos * ky)
        lo_c = lo_c * (1.0 / math.sqrt(NXY))
        lo_s = lo_s * (1.0 / math.sqrt(NXY))
        high_pos = lax.broadcasted_iota(jnp.int32, (16, SAMP), 0).astype(F32) * 8.0 + first
        hi_c, hi_s = fold_phase(high_pos * ky)
        even1, odd1 = k0[3] + k0[1], k0[3] - k0[1]
        even2, odd2 = k0[4] + k0[0], k0[4] - k0[0]
        for p in range(BAND // 8):
            r8 = slice(8 * p, 8 * p + 8)
            pr = k0[2] + even1 * wide(yconst[0, r8]) + even2 * wide(yconst[2, r8])
            pi = odd1 * wide(yconst[1, r8]) + odd2 * wide(yconst[3, r8])
            hc, hs = hi_c[p : p + 1], hi_s[p : p + 1]
            er = hc * lo_c - hs * lo_s
            es = hs * lo_c + hc * lo_s
            wr[k, 0, r8] = er * pr - es * pi
            wr[k, 1, r8] = er * pi + es * pr
        kh, kl = ke_h[band], ke_l[band]
        tbuf[...] = dot(jnp.concatenate([kh, kh], axis=1), cw[k]) + dot(kl, cw[k, 0:EXT])
        for c in range(2):
            vr = jnp.zeros((8, SAMP), F32)
            vi = jnp.zeros((8, SAMP), F32)
            for p in range(BAND // 8):
                tr = tbuf[c * BAND + 8 * p : c * BAND + 8 * p + 8]
                ti = tbuf[192 + c * BAND + 8 * p : 192 + c * BAND + 8 * p + 8]
                w_r, w_i = wr[k, 0, 8 * p : 8 * p + 8], wr[k, 1, 8 * p : 8 * p + 8]
                vr = vr + w_r * tr + w_i * ti
                vi = vi + w_r * ti - w_i * tr
            vr = jnp.sum(vr, axis=0, keepdims=True)
            vi = jnp.sum(vi, axis=0, keepdims=True)
            for b in range(half):
                vsend[k, c, b : b + 1] = vr[:, 128 * b : 128 * (b + 1)]
                vsend[k, c, half + b : half + b + 1] = vi[:, 128 * b : 128 * (b + 1)]
        for e in range(2):
            if (k, e) == (0, 0):
                continue
            c = (pair + e) % 2
            s, r = eight_to(k, e)
            vals[k, e] = remote(
                vsend.at[k, c], vrecv.at[k, e], val_s.at[k, e], val_r.at[k, e], slab_to=s, row_to=r
            )

    total = vsend[0, pair]
    for k, e in eight:
        vals[k, e].wait_recv()
        total = total + vrecv[k, e]
    value = 0.5 * total
    dens = dens_ref[...]
    weighted = value * jnp.concatenate([dens, dens], axis=0)
    wall[row, pair, 0:8] = weighted
    curv = jnp.sum(weighted * value, axis=0, keepdims=True) * 2.0
    coils = 2 * ys_n

    def lanes(tile):
        folded = tile[:, 0:128] + tile[:, 128:256] + tile[:, 256:384]
        return jnp.sum(folded, axis=0, keepdims=True)

    dd = lanes(dir_ref[0] * dir_ref[0] + dir_ref[1] * dir_ref[1])
    rr = lanes(res_ref[0] * res_ref[0] + res_ref[1] * res_ref[1])
    wall[row, pair, 8:9] = curv + dd * (damping / coils)
    wall[row, pair, 9:10] = rr * (1.0 / coils)
    wall[row, pair, 10:16] = jnp.zeros((6, 128), F32)
    wts = {}
    for k, e in eight:
        s, r = eight_to(k, e)
        wts[k, e] = remote(
            wall.at[row, pair], wall.at[row, pair], wt_s.at[k, e], wt_r.at[k, e], slab_to=s, row_to=r
        )

    for k in range(rows_n):
        band = (row + k) % rows_n
        for e in range(2):
            if (k, e) != (0, 0):
                wts[(rows_n - k) % rows_n, e].wait_recv()
        for c in range(2):
            w_re = jnp.concatenate([wall[band, c, b : b + 1] for b in range(half)], axis=1)
            w_im = jnp.concatenate([wall[band, c, half + b : half + b + 1] for b in range(half)], axis=1)
            for p in range(BAND // 16):
                m_r = wr[k, 0, 16 * p : 16 * p + 16]
                m_i = wr[k, 1, 16 * p : 16 * p + 16]
                re_h, re_l = halves(m_r * w_re - m_i * w_im)
                im_h, im_l = halves(m_r * w_im + m_i * w_re)
                here = slice(c * BAND + 16 * p, c * BAND + 16 * p + 16)
                there = slice(192 + c * BAND + 16 * p, 192 + c * BAND + 16 * p + 16)
                a_h[here] = re_h
                a_h[there] = im_h
                a_l[here] = re_l
                a_l[there] = im_l
        both = dot_nt(a_h[...], cw[k])
        out = both[:, :EXT] + both[:, EXT:] + dot_nt(a_l[...], cw[k, 0:EXT])
        high, low = halves(out)
        s_h[band, 0] = high[0:192]
        s_h[band, 1] = high[192:384]
        s_l[band, 0] = low[0:192]
        s_l[band, 1] = low[192:384]

    mine = jnp.zeros((8, 128), F32)
    for r in range(rows_n):
        for c in range(2):
            mine = mine + wall[r, c, 8:16]
    g1[group] = mine
    g1c = [
        remote(g1.at[group], g1.at[group], g1_s.at[k], g1_r.at[k],
               slab_to=(group + k) % groups_n + groups_n * pair)
        for k in range(1, groups_n)
    ]

    left_h = jnp.concatenate([s_h[j, q] for j in range(rows_n) for q in range(2)], axis=1)
    left_l = jnp.concatenate([s_l[j, q] for j in range(rows_n) for q in range(2)], axis=1)
    other = (1 - zl) * ys_n + yy
    zrc = []
    for b in range(BLOCKS):
        out = dot(left_h, bh_ref[b]) + dot(left_l, bh_ref[b]) + dot(left_h, bl_ref[b])
        cols = slice(128 * b, 128 * (b + 1))
        term_r = dir_ref[0, :, cols] * (damping / coils)
        term_i = dir_ref[1, :, cols] * (damping / coils)
        for c in range(2):
            sr = sens_ref[0, c, :, cols].astype(F32)
            si = sens_ref[1, c, :, cols].astype(F32)
            br = out[c * BAND : (c + 1) * BAND, :128]
            bi = out[c * BAND : (c + 1) * BAND, 128:]
            term_r = term_r + sr * br + si * bi
            term_i = term_i + sr * bi - si * br
        for g in range(24):
            tz[b, 0, g] = term_r[4 * g : 4 * g + 4]
            tz[b, 1, g] = term_i[4 * g : 4 * g + 4]
        zrc.append(remote(tz.at[b, 1 - zl], zrecv.at[b], zr_s.at[b], zr_r.at[b], coil_to=other))

    for copy in g1c:
        copy.wait_recv()
    mine = g1[0]
    for k in range(1, groups_n):
        mine = mine + g1[k]
    z1[zl] = mine
    z1c = remote(z1.at[zl], z1.at[zl], z1_s, z1_r, coil_to=other)

    yrc = {}
    for b in range(BLOCKS):
        zrc[b].wait_recv()
        ysum[b] = tz[b, zl] + zrecv[b]
        for k in range(1, ys_n):
            to = (yy + k) % ys_n
            yrc[b, k] = remote(
                ysum.at[b, pl.ds(3 * to, 3)], yrecv.at[b, k], yr_s.at[b, k], yr_r.at[b, k],
                coil_to=zl * ys_n + to,
            )
        if b == 0:
            z1c.wait_recv()
            y1[yy] = z1[0] + z1[1]
            y1c = [
                remote(y1.at[yy], y1.at[yy], y1_s.at[k], y1_r.at[k], coil_to=zl * ys_n + (yy + k) % ys_n)
                for k in range(1, ys_n)
            ]
    for copy in y1c:
        copy.wait_recv()
    mine = y1[0]
    for k in range(1, ys_n):
        mine = mine + y1[k]
    curvature = jnp.sum(mine[0:1], axis=1, keepdims=True)
    norm_now = jnp.sum(mine[1:2], axis=1, keepdims=True)
    step = norm_now / curvature

    left = jnp.zeros((4, 128), F32)
    yac = {}
    for b in range(BLOCKS):
        for k in range(1, ys_n):
            yrc[b, k].wait_recv()
        for g in range(3):
            acc = ysum[b, 3 * yy + g]
            for k in range(1, ys_n):
                acc = acc + yrecv[b, k, g]
            nbuf[b, zl, 3 * yy + g] = acc
            gap = rz[b, zl, 3 * yy + g] - step * acc
            left = left + gap * gap
        piece = nbuf.at[b, zl, pl.ds(3 * yy, 3)]
        for k in range(1, ys_n):
            yac[b, k] = remote(
                piece, piece, ya_s.at[b, k], ya_r.at[b, k], coil_to=zl * ys_n + (yy + k) % ys_n
            )
    left = jnp.sum(left, axis=0, keepdims=True)
    e2[row, pair] = jnp.broadcast_to(left, (8, 128))
    e2c = {}
    for k, e in eight:
        s, r = eight_to(k, e)
        e2c[k, e] = remote(
            e2.at[row, pair], e2.at[row, pair], e2_s.at[k, e], e2_r.at[k, e], slab_to=s, row_to=r
        )
    for k, e in eight:
        e2c[k, e].wait_recv()
    mine = jnp.zeros((8, 128), F32)
    for r in range(rows_n):
        for c in range(2):
            mine = mine + e2[r, c]
    g2[group] = mine
    g2c = [
        remote(g2.at[group], g2.at[group], g2_s.at[k], g2_r.at[k],
               slab_to=(group + k) % groups_n + groups_n * pair)
        for k in range(1, groups_n)
    ]

    zac = []
    for b in range(BLOCKS):
        for k in range(1, ys_n):
            yac[b, k].wait_recv()
        part = nbuf.at[b, zl]
        zac.append(remote(part, part, za_s.at[b], za_r.at[b], coil_to=other))

    for copy in g2c:
        copy.wait_recv()
    mine = g2[0]
    for k in range(1, groups_n):
        mine = mine + g2[k]
    z2[zl] = mine
    z2c = remote(z2.at[zl], z2.at[zl], z2_s, z2_r, coil_to=other)
    z2c.wait_recv()
    y2[yy] = z2[0] + z2[1]
    y2c = [
        remote(y2.at[yy], y2.at[yy], y2_s.at[k], y2_r.at[k], coil_to=zl * ys_n + (yy + k) % ys_n)
        for k in range(1, ys_n)
    ]
    for copy in y2c:
        copy.wait_recv()
    mine = y2[0]
    for k in range(1, ys_n):
        mine = mine + y2[k]
    norm_next = jnp.sum(mine[0:1], axis=1, keepdims=True)
    scal_ref[0:1] = jnp.broadcast_to(step, (1, 128))
    scal_ref[1:2] = jnp.broadcast_to(norm_next / norm_now, (1, 128))
    scal_ref[2:8] = jnp.zeros((6, 128), F32)

    for b in range(BLOCKS):
        zac[b].wait_recv()
        for plane in range(2):
            for g in range(12):
                n_ref[plane, 8 * g : 8 * g + 4, 128 * b : 128 * (b + 1)] = nbuf[b, plane, 2 * g]
                n_ref[plane, 8 * g + 4 : 8 * g + 8, 128 * b : 128 * (b + 1)] = nbuf[b, plane, 2 * g + 1]
    for copy in started:
        copy.wait_send()


def on_device(tables, rows_n, groups_n, ys_n, solution, residual, direction, sens, sample_cell, kern, density):
    dma = pltpu.SemaphoreType.DMA
    vmem = pltpu.VMEM
    eight = (rows_n, 2)
    scratch = [
        vmem((192, 768), BF16), vmem((192, 768), BF16),
        vmem((rows_n, 384, EXT), BF16), vmem((rows_n, 384, EXT), BF16),
        vmem((rows_n, 16, SAMP), F32),
        vmem((rows_n, 2 * EXT, SAMP), BF16),
        vmem((rows_n, 2, BAND, SAMP), F32),
        vmem((384, SAMP), F32),
        vmem((4, BAND, 128), F32),
        vmem((384, SAMP), BF16), vmem((384, SAMP), BF16),
        vmem((rows_n, 2, 192, EXT), BF16), vmem((rows_n, 2, 192, EXT), BF16),
        vmem((rows_n, 2, 8, 128), F32), vmem((rows_n, 2, 8, 128), F32),
        vmem((rows_n, 2, 16, 128), F32),
        vmem((BLOCKS, 2, 24, 4, 128), F32),
        vmem((BLOCKS, 24, 4, 128), F32),
        vmem((BLOCKS, ys_n, 3, 4, 128), F32),
        vmem((BLOCKS, 24, 4, 128), F32),
        vmem((BLOCKS, 2, 24, 4, 128), F32),
        vmem((BLOCKS, 2, 24, 4, 128), F32),
        vmem((groups_n, 8, 128), F32), vmem((2, 8, 128), F32), vmem((ys_n, 8, 128), F32),
        vmem((rows_n, 2, 8, 128), F32),
        vmem((groups_n, 8, 128), F32), vmem((2, 8, 128), F32), vmem((ys_n, 8, 128), F32),
    ]
    one = (groups_n,), (groups_n,), (), (), (ys_n,), (ys_n,)
    for shape in (
        ((rows_n,), (rows_n,), eight, eight, eight, eight) + one + (eight, eight) + one
        + ((BLOCKS,), (BLOCKS,)) + ((BLOCKS, ys_n),) * 4 + ((BLOCKS,), (BLOCKS,))
    ):
        scratch.append(dma(shape) if shape else dma)
    spec = pl.BlockSpec(memory_space=pltpu.VMEM)
    normal, scal = pl.pallas_call(
        functools.partial(kernel, rows_n, groups_n, ys_n),
        out_shape=(
            jax.ShapeDtypeStruct((2, BAND, NXY), F32),
            jax.ShapeDtypeStruct((8, 128), F32),
        ),
        in_specs=[spec] * 10,
        out_specs=(spec, spec),
        scratch_shapes=scratch,
        compiler_params=pltpu.CompilerParams(
            collective_id=0, has_side_effects=True, vmem_limit_bytes=48 * 1024 * 1024
        ),
    )(
        direction[:, 0], residual[:, 0], sens[:, :, 0],
        sample_cell.reshape(1, SAMP), kern, density.reshape(4, 128), *tables,
    )
    step, ratio = scal[0, 0], scal[1, 0]
    normal = normal[:, None]
    solution_next = solution + step * direction
    residual_next = residual - step * normal
    direction_next = residual_next + ratio * direction
    return solution_next, residual_next, direction_next


def solution(mesh):
    rows_n = mesh.shape["row"]
    groups_n = mesh.shape["slab"] // 2
    ys_n = mesh.shape["coil"] // 2
    tables = transform_tables(rows_n)

    def whole(*args):
        return on_device([jnp.asarray(t) for t in tables], rows_n, groups_n, ys_n, *args)

    image = P(None, "slab", "row", None)
    return jax.shard_map(
        whole,
        mesh=mesh,
        in_specs=(
            image, image, image, P(None, "coil", "slab", "row", None),
            P("row"), P(None, None, "row"), P("row"),
        ),
        out_specs=(image, image, image),
        check_vma=False,
    )
```

time: 467 us -> 78.4 us (0.17)
  the two profiles are of different devices: /device:TPU:16 before, /device:TPU:1 now
where the time goes in v1:
time: 78.4 us; the launch traced here: 77.4 us
  Pallas kernels  63.5 us (81%)
  local copies, waits for them, and re-layouts  9.78 us (12%)
  other arithmetic  3.5 us (4%)
    pallas_call x1, Pallas kernels, on_device(): pl.pallas_call(functools.partial(kernel, rows_n, groups_n, ys_n), out_sha...  63.5 us
    unnamed x19, local copies, waits for them, and re-layouts  9.21 us
    unnamed x1, other arithmetic  2.13 us

profile of v1, /device:TPU:1, one launch (start us, length us, event | category | flops | bytes accessed | tf_op | source)
XLA Modules:
  0.0 77.4 jit_solution(14815426149911665998)
XLA Ops:
  0.6 0.7 copy.14.kern_ref
  1.4 0.0 copy-start
  1.4 1.0 %copy-done = f32[2,1,96,384]{3,2,1,0:T(8,128)S(1)} copy-done((f32[2,1,96,384]{3,2,1,0:T(8,128)S(1)}, f32[2,1,96,384]{3,2,1,0:T(8,128)}, u32[]{:S(2)}) %copy-start) | copy-done | bytes 294936
  2.3 0.0 copy-start.1
  2.3 1.4 %copy-done.1 = bf16[3,1024,256]{2,1,0:T(8,128)(2,1)S(1)} copy-done((bf16[3,1024,256]{2,1,0:T(8,128)(2,1)S(1)}, bf16[3,1024,256]{2,1,0:T(8,128)(2,1)}, u32[]{:S(2)}) %copy-start.1) | copy-done | bytes 1572888
  3.7 0.0 copy-start.2
  3.7 1.4 %copy-done.2 = bf16[4,768,256]{2,1,0:T(8,128)(2,1)S(1)} copy-done((bf16[4,768,256]{2,1,0:T(8,128)(2,1)S(1)}, bf16[4,768,256]{2,1,0:T(8,128)(2,1)}, u32[]{:S(2)}) %copy-start.2) | copy-done | bytes 1572888
  5.1 0.0 copy-start.3
  5.1 1.4 %copy-done.3 = bf16[4,768,256]{2,1,0:T(8,128)(2,1)S(1)} copy-done((bf16[4,768,256]{2,1,0:T(8,128)(2,1)S(1)}, bf16[4,768,256]{2,1,0:T(8,128)(2,1)}, u32[]{:S(2)}) %copy-start.3) | copy-done | bytes 1572888
  6.6 0.0 copy-start.4
  6.6 1.0 %copy-done.4 = f32[2,1,96,384]{3,2,1,0:T(8,128)S(1)} copy-done((f32[2,1,96,384]{3,2,1,0:T(8,128)S(1)}, f32[2,1,96,384]{3,2,1,0:T(8,128)}, u32[]{:S(2)}) %copy-start.4) | copy-done | bytes 294936
  7.5 0.0 copy-start.5
  7.5 1.0 %copy-done.5 = bf16[2,2,1,96,384]{4,3,2,1,0:T(8,128)(2,1)S(1)} copy-done((bf16[2,2,1,96,384]{4,3,2,1,0:T(8,128)(2,1)S(1)}, bf16[2,2,1,96,384]{4,3,2,1,0:T(8,128)(2,1)}, u32[]{:S(2)}) %copy-start.5) | copy-done | bytes 294936
  8.5 0.0 copy-start.6
  8.5 0.7 copy-done.6
  9.2 0.0 copy-start.7
  9.2 0.7 copy-done.7
  9.8 63.5 %shard_map.130 = (f32[2,96,384]{2,1,0:T(8,128)S(1)}, f32[8,128]{1,0:T(8,128)S(1)}) custom-call(f32[2,96,384]{2,1,0:T(8,128)S(1)} %bitcast.29, f32[2,96,384]{2,1,0:T(8,128)S(1)} %bitcast.30, bf16[2,2,96,384]{3,2,1,0:T(8,128)(2,1)S(1)} %bitcast.31, s32[1,512]{1,0:T(1,128)S(1)} %bitcast.32, f32[2,5,512]{2,1,0:T(8,128)S(1)} %copy.14.kern_ref, ...), custom_call_target="tpu_custom_call" | custom-call | tf_op jit(solution)/shard_map/pallas_call | solution.py:488
  73.3 0.0 copy-start.8
  73.3 0.6 fusion.3
  73.9 2.1 %fusion.1 = (f32[2,1,96,384]{3,2,1,0:T(8,128)}, f32[2,1,96,384]{3,2,1,0:T(8,128)}) fusion(f32[2,1,96,384]{3,2,1,0:T(8,128)S(1)} %copy-done, f32[]{:T(128)} %bitcast.9, f32[2,96,384]{2,1,0:T(8,128)S(1)} %get-tuple-element.6, f32[]{:T(128)} %bitcast.5, f32[2,1,96,384]{3,2,1,0:T(8,128)S(1)} %copy-done.4), kind=kLoop, calls=%fused_computation.2 | loop fusion | flops 294912 | bytes 1474568
  76.0 0.0 copy-done.8
  76.0 1.4 %multiply_add_fusion = f32[2,1,96,384]{3,2,1,0:T(8,128)} fusion(f32[2,1,96,384]{3,2,1,0:T(8,128)S(1)} %copy-done.8, f32[2,1,96,384]{3,2,1,0:T(8,128)S(1)} %copy-done, f32[]{:T(128)} %bitcast.5), kind=kLoop, calls=%fused_computation.4 | loop fusion | flops 147456 | bytes 884740 | tf_op jit(solution)/shard_map/add | solution.py:506
Async XLA Ops:
  1.4 1.0 %copy-start = (f32[2,1,96,384]{3,2,1,0:T(8,128)S(1)}, f32[2,1,96,384]{3,2,1,0:T(8,128)}, u32[]{:S(2)}) copy-start(f32[2,1,96,384]{3,2,1,0:T(8,128)} %param.13) | copy-start | bytes 884740
  2.3 1.4 %copy-start.1 = (bf16[3,1024,256]{2,1,0:T(8,128)(2,1)S(1)}, bf16[3,1024,256]{2,1,0:T(8,128)(2,1)}, u32[]{:S(2)}) copy-start(bf16[3,1024,256]{2,1,0:T(8,128)(2,1)} %constant.10.clone.bh_ref) | copy-start | bytes 4718596
  3.7 1.4 %copy-start.2 = (bf16[4,768,256]{2,1,0:T(8,128)(2,1)S(1)}, bf16[4,768,256]{2,1,0:T(8,128)(2,1)}, u32[]{:S(2)}) copy-start(bf16[4,768,256]{2,1,0:T(8,128)(2,1)} %constant.9.clone.fl_ref) | copy-start | bytes 4718596
  5.1 1.4 %copy-start.3 = (bf16[4,768,256]{2,1,0:T(8,128)(2,1)S(1)}, bf16[4,768,256]{2,1,0:T(8,128)(2,1)}, u32[]{:S(2)}) copy-start(bf16[4,768,256]{2,1,0:T(8,128)(2,1)} %constant.8.clone.fh_ref) | copy-start | bytes 4718596
  6.6 1.0 %copy-start.4 = (f32[2,1,96,384]{3,2,1,0:T(8,128)S(1)}, f32[2,1,96,384]{3,2,1,0:T(8,128)}, u32[]{:S(2)}) copy-start(f32[2,1,96,384]{3,2,1,0:T(8,128)} %param.12) | copy-start | bytes 884740
  7.5 1.0 %copy-start.5 = (bf16[2,2,1,96,384]{4,3,2,1,0:T(8,128)(2,1)S(1)}, bf16[2,2,1,96,384]{4,3,2,1,0:T(8,128)(2,1)}, u32[]{:S(2)}) copy-start(bf16[2,2,1,96,384]{4,3,2,1,0:T(8,128)(2,1)} %param.14) | copy-start | bytes 884740
  8.5 0.7 copy-start.6
  9.2 0.7 copy-start.7
  73.3 2.7 %copy-start.8 = (f32[2,1,96,384]{3,2,1,0:T(8,128)S(1)}, f32[2,1,96,384]{3,2,1,0:T(8,128)}, u32[]{:S(2)}) copy-start(f32[2,1,96,384]{3,2,1,0:T(8,128)} %param.11) | copy-start | bytes 884740

commit v2 on v1

v2 whole, which is shorter than its diff:
```python
import functools
import math

import jax
import jax.numpy as jnp
import ml_dtypes
import numpy as np
from jax import lax
from jax.experimental import pallas as pl
from jax.experimental.pallas import tpu as pltpu
from jax.sharding import PartitionSpec as P

damping = 0.05
NXY = 384
BAND = 96
EXT = 128
HALO = 2
SAMP = 512
TAPS = 5
BLOCKS = 3
F32 = jnp.float32
BF16 = jnp.bfloat16
MESH = pl.DeviceIdType.MESH


def split_table(table):
    high = table.astype(np.float32).astype(ml_dtypes.bfloat16)
    low = (table - high.astype(np.float64)).astype(np.float32).astype(ml_dtypes.bfloat16)
    return high, low


def transform_tables(bands):
    x = np.arange(NXY)
    forward = np.zeros((bands, 2 * NXY, 2 * EXT))
    inverse = np.zeros((BLOCKS, bands * 2 * EXT, 256))
    scale = 1.0 / math.sqrt(NXY)
    for band in range(bands):
        k = (band * BAND - HALO + np.arange(EXT)) % NXY
        angle = (x[:, None] * k[None, :] % NXY) * (2.0 * math.pi / NXY)
        cosine, sine = np.cos(angle) * scale, np.sin(angle) * scale
        forward[band] = np.block([[cosine, -sine], [sine, cosine]])
        back = np.block([[cosine.T, sine.T], [-sine.T, cosine.T]])
        rows = slice(band * 2 * EXT, (band + 1) * 2 * EXT)
        for block in range(BLOCKS):
            cols = slice(block * 128, (block + 1) * 128)
            inverse[block, rows, :128] = back[:, :NXY][:, cols]
            inverse[block, rows, 128:] = back[:, NXY:][:, cols]
    return split_table(forward) + split_table(inverse)


def halves(value):
    high = value.astype(BF16)
    return high, (value - high.astype(F32)).astype(BF16)


def fold_phase(index):
    turn = index - NXY * jnp.floor(index * (1.0 / NXY) + 0.5)
    size = jnp.abs(turn)

    def sine_quarter(u):
        t = u * (2.0 * math.pi / NXY)
        q = t * t
        p = 1.0 / 6227020800.0
        for c in (-1.0 / 39916800.0, 1.0 / 362880.0, -1.0 / 5040.0, 1.0 / 120.0, -1.0 / 6.0, 1.0):
            p = p * q + c
        return p * t

    quarter = NXY // 4
    cosine = sine_quarter(quarter - size)
    sine = sine_quarter(quarter - jnp.abs(size - quarter))
    return cosine, jnp.where(turn < 0.0, -sine, sine)


def dot(a, b):
    return lax.dot_general(a, b, (((1,), (0,)), ((), ())), preferred_element_type=F32)


def dot_nt(a, b):
    return lax.dot_general(a, b, (((1,), (1,)), ((), ())), preferred_element_type=F32)


def kernel(
    rows_n, groups_n, ys_n,
    dir_in, res_in, sol_in, sens_in, cell_in, kern_in, dens_in,
    fh_in, fl_in, bh_in, bl_in,
    sol_out, res_out, dir_out,
    dir_ref, res_ref, sol_ref, sens_ref, cell_ref, dens_ref,
    fh_ref, fl_ref, bh_ref, bl_ref, in_sem,
    sol_buf, res_buf, dir_buf, out_sem,
    lhs_h, lhs_l, ke_h, ke_l, sinfo, cw, wr, tbuf, yconst, a_h, a_l, s_h, s_l,
    vsend, vrecv, wall, tz, zrecv, ysum, yrecv, nb, g1, e2, g2, y2,
    info_s, info_r, val_s, val_r, wt_s, wt_r, g1_s, g1_r, zr_s, zr_r, yr_s, yr_r,
    e2_s, e2_r, ya_s, ya_r, za_s, za_r, g2_s, g2_r, y2_s, y2_r,
):
    slab = lax.axis_index("slab")
    coil = lax.axis_index("coil")
    row = lax.axis_index("row")
    pair = slab // groups_n
    group = slab % groups_n
    zl = coil // ys_n
    yy = coil % ys_n
    half = SAMP // 128
    coils = 2 * ys_n
    orders = [0, 1, rows_n - 1] + list(range(2, rows_n - 1))
    ins = [
        pltpu.make_async_copy(src, dst, in_sem.at[i])
        for i, (src, dst) in enumerate((
            (cell_in, cell_ref), (kern_in, sinfo.at[row, pl.ds(0, 8 * TAPS)]), (dir_in, dir_ref), (sens_in, sens_ref),
            (fh_in, fh_ref), (fl_in, fl_ref), (res_in, res_ref), (dens_in, dens_ref),
            (sol_in, sol_ref), (bh_in, bh_ref), (bl_in, bl_ref),
        ))
    ]
    for copy in ins[:9]:
        copy.start()

    def remote(src, dst, send, recv, slab_to=None, coil_to=None, row_to=None):
        target = (
            slab if slab_to is None else slab_to,
            coil if coil_to is None else coil_to,
            row if row_to is None else row_to,
        )
        copy = pltpu.make_async_remote_copy(
            src_ref=src, dst_ref=dst, send_sem=send, recv_sem=recv,
            device_id=target, device_id_type=MESH,
        )
        copy.start()
        started.append(copy)
        return copy

    started = []

    def drain():
        for copy in started:
            copy.wait_send()
        started.clear()

    eight = [(k, e) for k in range(rows_n) for e in range(2) if (k, e) != (0, 0)]

    def eight_to(k, e):
        return (group + groups_n * ((pair + e) % 2), (row + k) % rows_n)

    barrier = pltpu.get_barrier_semaphore()
    count = 0
    for k, e in eight:
        s, r = eight_to(k, e)
        pl.semaphore_signal(barrier, inc=1, device_id=(s, coil, r), device_id_type=MESH)
        count += 1
    across = [(k, e) for k in range(groups_n) for e in range(2) if (k, e) != (0, 0)]

    def across_to(k, e):
        return (group + k) % groups_n + groups_n * pair, ((zl + e) % 2) * ys_n + yy

    for k, e in across:
        s, c = across_to(k, e)
        pl.semaphore_signal(barrier, inc=1, device_id=(s, c, row), device_id_type=MESH)
        count += 1

    def along_y(k):
        return zl * ys_n + (yy + k) % ys_n

    for k in range(1, ys_n):
        pl.semaphore_signal(barrier, inc=1, device_id=(slab, along_y(k), row), device_id_type=MESH)
        count += 1
    near = sorted(range(1, ys_n), key=lambda k: min(k, ys_n - k))

    first = (row * BAND).astype(F32)
    ypos = lax.broadcasted_iota(jnp.int32, (BAND, 128), 0).astype(F32) + first
    c1, s1 = fold_phase(ypos)
    yconst[0] = c1
    yconst[1] = s1
    yconst[2] = 2.0 * c1 * c1 - 1.0
    yconst[3] = 2.0 * s1 * c1

    ins[0].wait()
    ins[1].wait()
    sinfo[row, 8 * TAPS : 8 * TAPS + 4] = cell_ref[...].astype(F32)

    pl.semaphore_wait(barrier, count)
    info = [None] + [
        remote(sinfo.at[row], sinfo.at[row], info_s.at[k], info_r.at[k], row_to=(row + k) % rows_n)
        for k in range(1, rows_n)
    ]

    def wide(tile):
        return jnp.concatenate([tile] * half, axis=1)

    def tables(k):
        band = (row + k) % rows_n
        cell = jnp.concatenate([sinfo[band, 8 * TAPS + b : 8 * TAPS + b + 1] for b in range(half)], axis=1)
        kxs = jnp.floor((cell + 0.5) * (1.0 / NXY))
        ky = cell - NXY * kxs
        k0, k1 = [
            [
                jnp.concatenate(
                    [sinfo[band, 8 * t + 2 * b + q : 8 * t + 2 * b + q + 1] for b in range(half)], axis=1
                )
                for t in range(TAPS)
            ]
            for q in range(2)
        ]
        cells = lax.broadcasted_iota(jnp.int32, (16, SAMP), 0).astype(F32)
        for g in range(8):
            if g < 7:
                offset = cells + (16.0 * g) - kxs
                weight = jnp.where(offset == 4.0, k1[4], 0.0)
                for t in range(3, -1, -1):
                    weight = jnp.where(offset == float(t), k1[t], weight)
                high, low = halves(weight)
            else:
                high = low = jnp.zeros((16, SAMP), BF16)
            cw[k, 16 * g : 16 * g + 16] = high
            cw[k, EXT + 16 * g : EXT + 16 * g + 16] = low
        low_pos = lax.broadcasted_iota(jnp.int32, (8, SAMP), 0).astype(F32)
        lo_c, lo_s = fold_phase(low_pos * ky)
        lo_c = lo_c * (1.0 / math.sqrt(NXY))
        lo_s = lo_s * (1.0 / math.sqrt(NXY))
        high_pos = lax.broadcasted_iota(jnp.int32, (16, SAMP), 0).astype(F32) * 8.0 + first
        hi_c, hi_s = fold_phase(high_pos * ky)
        even1, odd1 = k0[3] + k0[1], k0[3] - k0[1]
        even2, odd2 = k0[4] + k0[0], k0[4] - k0[0]
        for p in range(BAND // 8):
            r8 = slice(8 * p, 8 * p + 8)
            pr = k0[2] + even1 * wide(yconst[0, r8]) + even2 * wide(yconst[2, r8])
            pi = odd1 * wide(yconst[1, r8]) + odd2 * wide(yconst[3, r8])
            hc, hs = hi_c[p : p + 1], hi_s[p : p + 1]
            er = hc * lo_c - hs * lo_s
            es = hs * lo_c + hc * lo_s
            wr[k, 0, r8] = er * pr - es * pi
            wr[k, 1, r8] = er * pi + es * pr

    tables(0)

    ins[2].wait()
    ins[3].wait()
    for c in range(2):
        sr, si = sens_ref[0, c].astype(F32), sens_ref[1, c].astype(F32)
        dr, di = dir_ref[0], dir_ref[1]
        re_h, re_l = halves(sr * dr - si * di)
        im_h, im_l = halves(sr * di + si * dr)
        here = slice(c * BAND, (c + 1) * BAND)
        lhs_h[here, 0:NXY] = re_h
        lhs_h[here, NXY:] = im_h
        lhs_l[here, 0:NXY] = re_l
        lhs_l[here, NXY:] = im_l

    ins[4].wait()
    ins[5].wait()
    for copy in ins[9:]:
        copy.start()
    for band in range(rows_n):
        out = dot(lhs_h[...], fh_ref[band])
        out = out + dot(lhs_l[...], fh_ref[band])
        out = out + dot(lhs_h[...], fl_ref[band])
        high, low = halves(out)
        ke_h[band, 0:192] = high[:, :EXT]
        ke_h[band, 192:384] = high[:, EXT:]
        ke_l[band, 0:192] = low[:, :EXT]
        ke_l[band, 192:384] = low[:, EXT:]

    vals = {}
    for k in orders:
        band = (row + k) % rows_n
        if k:
            info[rows_n - k].wait_recv()
            tables(k)
        kh, kl = ke_h[band], ke_l[band]
        tbuf[...] = dot(jnp.concatenate([kh, kh], axis=1), cw[k]) + dot(kl, cw[k, 0:EXT])
        for c in range(2):
            vr = jnp.zeros((8, SAMP), F32)
            vi = jnp.zeros((8, SAMP), F32)
            for p in range(BAND // 8):
                tr = tbuf[c * BAND + 8 * p : c * BAND + 8 * p + 8]
                ti = tbuf[192 + c * BAND + 8 * p : 192 + c * BAND + 8 * p + 8]
                w_r, w_i = wr[k, 0, 8 * p : 8 * p + 8], wr[k, 1, 8 * p : 8 * p + 8]
                vr = vr + w_r * tr + w_i * ti
                vi = vi + w_r * ti - w_i * tr
            vr = jnp.sum(vr, axis=0, keepdims=True)
            vi = jnp.sum(vi, axis=0, keepdims=True)
            for b in range(half):
                vsend[k, c, b : b + 1] = vr[:, 128 * b : 128 * (b + 1)]
                vsend[k, c, half + b : half + b + 1] = vi[:, 128 * b : 128 * (b + 1)]
        for e in range(2):
            if (k, e) == (0, 0):
                continue
            c = (pair + e) % 2
            s, r = eight_to(k, e)
            vals[k, e] = remote(
                vsend.at[k, c], vrecv.at[k, e], val_s.at[k, e], val_r.at[k, e], slab_to=s, row_to=r
            )

    total = vsend[0, pair]
    for k, e in eight:
        vals[k, e].wait_recv()
        total = total + vrecv[k, e]
    value = 0.5 * total
    ins[7].wait()
    dens = dens_ref[...]
    weighted = value * jnp.concatenate([dens, dens], axis=0)
    wall[row, pair, 0:8] = weighted
    curv = jnp.sum(weighted * value, axis=0, keepdims=True) * 2.0

    def lanes(tile):
        folded = tile[:, 0:128] + tile[:, 128:256] + tile[:, 256:384]
        return jnp.sum(folded, axis=0, keepdims=True)

    dd = lanes(dir_ref[0] * dir_ref[0] + dir_ref[1] * dir_ref[1])
    ins[6].wait()
    rr = lanes(res_ref[0] * res_ref[0] + res_ref[1] * res_ref[1])
    wall[row, pair, 8:9] = curv + dd * (damping / coils)
    wall[row, pair, 9:10] = rr * (1.0 / coils)
    wall[row, pair, 10:16] = jnp.zeros((6, 128), F32)
    wts = {}
    for k, e in eight:
        s, r = eight_to(k, e)
        wts[k, e] = remote(
            wall.at[row, pair], wall.at[row, pair], wt_s.at[k, e], wt_r.at[k, e], slab_to=s, row_to=r
        )

    for k in orders:
        band = (row + k) % rows_n
        for e in range(2):
            if (k, e) != (0, 0):
                wts[(rows_n - k) % rows_n, e].wait_recv()
        for c in range(2):
            w_re = jnp.concatenate([wall[band, c, b : b + 1] for b in range(half)], axis=1)
            w_im = jnp.concatenate([wall[band, c, half + b : half + b + 1] for b in range(half)], axis=1)
            for p in range(BAND // 16):
                m_r = wr[k, 0, 16 * p : 16 * p + 16]
                m_i = wr[k, 1, 16 * p : 16 * p + 16]
                re_h, re_l = halves(m_r * w_re - m_i * w_im)
                im_h, im_l = halves(m_r * w_im + m_i * w_re)
                here = slice(c * BAND + 16 * p, c * BAND + 16 * p + 16)
                there = slice(192 + c * BAND + 16 * p, 192 + c * BAND + 16 * p + 16)
                a_h[here] = re_h
                a_h[there] = im_h
                a_l[here] = re_l
                a_l[there] = im_l
        both = dot_nt(a_h[...], cw[k])
        out = both[:, :EXT] + both[:, EXT:] + dot_nt(a_l[...], cw[k, 0:EXT])
        high, low = halves(out)
        s_h[band, 0] = high[0:192]
        s_h[band, 1] = high[192:384]
        s_l[band, 0] = low[0:192]
        s_l[band, 1] = low[192:384]

    mine = jnp.zeros((8, 128), F32)
    for r in range(rows_n):
        for c in range(2):
            mine = mine + wall[r, c, 8:16]

    def to_across(buf, send, recv):
        copies = []
        for k, e in across:
            s, c = across_to(k, e)
            copies.append(
                remote(buf.at[group, zl], buf.at[group, zl], send.at[k, e], recv.at[k, e], slab_to=s, coil_to=c)
            )
        return copies

    def total_of(buf, first, second):
        mine = jnp.zeros((8, 128), F32)
        for i in range(first):
            for j in range(second):
                mine = mine + buf[i, j]
        return mine

    g1[group, zl] = mine
    g1c = to_across(g1, g1_s, g1_r)

    left_h = jnp.concatenate([s_h[j, q] for j in range(rows_n) for q in range(2)], axis=1)
    left_l = jnp.concatenate([s_l[j, q] for j in range(rows_n) for q in range(2)], axis=1)
    other = (1 - zl) * ys_n + yy
    zrc = []
    ins[9].wait()
    ins[10].wait()
    for b in range(BLOCKS):
        out = dot(left_h, bh_ref[b]) + dot(left_l, bh_ref[b]) + dot(left_h, bl_ref[b])
        cols = slice(128 * b, 128 * (b + 1))
        term_r = dir_ref[0, :, cols] * (damping / coils)
        term_i = dir_ref[1, :, cols] * (damping / coils)
        for c in range(2):
            sr = sens_ref[0, c, :, cols].astype(F32)
            si = sens_ref[1, c, :, cols].astype(F32)
            br = out[c * BAND : (c + 1) * BAND, :128]
            bi = out[c * BAND : (c + 1) * BAND, 128:]
            term_r = term_r + sr * br + si * bi
            term_i = term_i + sr * bi - si * br
        for g in range(24):
            tz[b, 0, g] = term_r[4 * g : 4 * g + 4]
            tz[b, 1, g] = term_i[4 * g : 4 * g + 4]
        zrc.append(remote(tz.at[b, 1 - zl], zrecv.at[b], zr_s.at[b], zr_r.at[b], coil_to=other))
    for copy in g1c:
        copy.wait_recv()
    mine = total_of(g1, groups_n, 2)
    for i in range(ys_n):
        ysum[i, 36:40] = mine[0:4]
    for b in range(BLOCKS):
        zrc[b].wait_recv()
        for i in range(ys_n):
            for g in range(3):
                at = 12 * b + 4 * g
                ysum[i, at : at + 4] = tz[b, zl, 3 * i + g] + zrecv[b, 3 * i + g]
    yrc = []
    for k in reversed(near):
        to = (yy + k) % ys_n
        yrc.append(remote(ysum.at[to], yrecv.at[yy], yr_s.at[k], yr_r.at[k], coil_to=along_y(k)))
    yrecv[yy] = ysum[yy]
    drain()
    for copy in yrc:
        copy.wait_recv()
    piece = yrecv[0]
    for c in range(1, ys_n):
        piece = piece + yrecv[c]
    curvature = jnp.sum(piece[36:37], axis=1, keepdims=True)
    norm_now = jnp.sum(piece[37:38], axis=1, keepdims=True)
    step = norm_now / curvature

    left = jnp.zeros((12, 128), F32)
    for b in range(BLOCKS):
        rows = res_ref[zl, pl.ds(pl.multiple_of(8 * (12 * yy // 8), 8), 16), 128 * b : 128 * (b + 1)]
        own = jnp.where(yy % 2 == 1, rows[4:16], rows[0:12])
        gap = own - step * piece[12 * b : 12 * b + 12]
        left = left + gap * gap
    nb[coil, 0:36] = piece[0:36]
    nb[coil, 36:40] = jnp.zeros((4, 128), F32)
    left = jnp.concatenate([left[0:4] + left[4:8] + left[8:12], jnp.zeros((4, 128), F32)], axis=0)
    e2[row, pair] = left
    e2c = []
    for k, e in eight:
        s, r = eight_to(k, e)
        e2c.append(
            remote(e2.at[row, pair], e2.at[row, pair], e2_s.at[k, e], e2_r.at[k, e], slab_to=s, row_to=r)
        )
    yac = {
        k: remote(nb.at[coil], nb.at[coil], ya_s.at[k], ya_r.at[k], coil_to=along_y(k)) for k in near
    }

    def forward(k):
        part = nb.at[zl * ys_n + (yy - k + ys_n) % ys_n]
        return remote(part, part, za_s.at[k], za_r.at[k], coil_to=other)

    zac = [forward(0)]
    ins[8].wait()
    sol_buf[...] = sol_ref[...] + step * dir_ref[...]
    outs = [
        pltpu.make_async_copy(src, dst, out_sem.at[i])
        for i, (src, dst) in enumerate(((sol_buf, sol_out), (res_buf, res_out), (dir_buf, dir_out)))
    ]
    outs[0].start()
    for copy in e2c:
        copy.wait_recv()
    g2[group, zl] = total_of(e2, rows_n, 2)
    g2c = to_across(g2, g2_s, g2_r)
    for k in near:
        yac[k].wait_recv()
        zac.append(forward(k))
    for copy in g2c:
        copy.wait_recv()
    y2[yy] = total_of(g2, groups_n, 2)
    y2c = [
        remote(y2.at[yy], y2.at[yy], y2_s.at[k], y2_r.at[k], coil_to=along_y(k)) for k in range(1, ys_n)
    ]
    for copy in zac:
        copy.wait_recv()
    for b in range(BLOCKS):
        cols = slice(128 * b, 128 * (b + 1))
        for plane in range(2):
            for g in range(12):
                here = slice(8 * g, 8 * g + 8)
                parts = []
                for u in (2 * g, 2 * g + 1):
                    at = 12 * b + 4 * (u % 3)
                    parts.append(nb[plane * ys_n + u // 3, at : at + 4])
                normal = jnp.concatenate(parts, axis=0)
                res_buf[plane, here, cols] = res_ref[plane, here, cols] - step * normal
    outs[1].start()
    for copy in y2c:
        copy.wait_recv()
    mine = y2[0]
    for c in range(1, ys_n):
        mine = mine + y2[c]
    folded = jnp.sum(mine[0:4], axis=0, keepdims=True)
    ratio = jnp.sum(folded, axis=1, keepdims=True) / norm_now
    dir_buf[...] = res_buf[...] + ratio * dir_ref[...]
    outs[2].start()
    drain()
    for copy in outs:
        copy.wait()


def put_kernel(a_ref, b_ref, c_ref, a_out, b_out, c_out, a_buf, b_buf, c_buf, load_sems, store_sems):
    refs = ((a_ref, a_buf, a_out), (b_ref, b_buf, b_out), (c_ref, c_buf, c_out))
    loads = [pltpu.make_async_copy(src, buf, load_sems.at[i]) for i, (src, buf, _) in enumerate(refs)]
    stores = [pltpu.make_async_copy(buf, dst, store_sems.at[i]) for i, (_, buf, dst) in enumerate(refs)]
    for copy in loads:
        copy.start()
    for load, store in zip(loads, stores):
        load.wait()
        store.start()
    for copy in stores:
        copy.wait()


def on_device(tables, rows_n, groups_n, ys_n, solution, residual, direction, sens, sample_cell, kern, density):
    dma = pltpu.SemaphoreType.DMA
    vmem = pltpu.VMEM
    eight = (rows_n, 2)
    image = (2, BAND, NXY)
    scratch = [
        vmem(image, F32), vmem(image, F32), vmem(image, F32), vmem((2,) + image, BF16),
        vmem((4, 128), jnp.int32), vmem((4, 128), F32),
        vmem(tables[0].shape, BF16), vmem(tables[1].shape, BF16),
        vmem(tables[2].shape, BF16), vmem(tables[3].shape, BF16), dma((11,)),
        vmem(image, F32), vmem(image, F32), vmem(image, F32), dma((3,)),
        vmem((192, 768), BF16), vmem((192, 768), BF16),
        vmem((rows_n, 384, EXT), BF16), vmem((rows_n, 384, EXT), BF16),
        vmem((rows_n, 48, 128), F32),
        vmem((rows_n, 2 * EXT, SAMP), BF16),
        vmem((rows_n, 2, BAND, SAMP), F32),
        vmem((384, SAMP), F32),
        vmem((4, BAND, 128), F32),
        vmem((384, SAMP), BF16), vmem((384, SAMP), BF16),
        vmem((rows_n, 2, 192, EXT), BF16), vmem((rows_n, 2, 192, EXT), BF16),
        vmem((rows_n, 2, 8, 128), F32), vmem((rows_n, 2, 8, 128), F32),
        vmem((rows_n, 2, 16, 128), F32),
        vmem((BLOCKS, 2, 24, 4, 128), F32), vmem((BLOCKS, 24, 4, 128), F32),
        vmem((ys_n, 40, 128), F32), vmem((ys_n, 40, 128), F32), vmem((2 * ys_n, 40, 128), F32),
        vmem((groups_n, 2, 8, 128), F32), vmem((rows_n, 2, 8, 128), F32),
        vmem((groups_n, 2, 8, 128), F32), vmem((ys_n, 8, 128), F32),
    ]
    few, cross, ys, blocks = (rows_n,), (groups_n, 2), (ys_n,), (BLOCKS,)
    for shape in (few, eight, eight, cross, blocks, ys, eight, ys, ys, cross, ys):
        scratch.append(dma(shape))
        scratch.append(dma(shape))
    far = pl.BlockSpec(memory_space=pl.ANY)
    shapes = (jax.ShapeDtypeStruct(image, F32),) * 3
    taps = kern.reshape(2, TAPS, 4, 128).transpose(1, 2, 0, 3).reshape(8 * TAPS, 128)
    outs = pl.pallas_call(
        functools.partial(kernel, rows_n, groups_n, ys_n),
        out_shape=shapes,
        in_specs=[far] * 11,
        out_specs=(far,) * 3,
        scratch_shapes=scratch,
        compiler_params=pltpu.CompilerParams(
            collective_id=0, has_side_effects=True, vmem_limit_bytes=56000 * 1024
        ),
    )(
        direction[:, 0], residual[:, 0], solution[:, 0], sens[:, :, 0],
        sample_cell.reshape(4, 128), taps, density.reshape(4, 128), *tables,
    )
    outs = pl.pallas_call(
        put_kernel,
        out_shape=shapes,
        in_specs=[far] * 3,
        out_specs=(far,) * 3,
        scratch_shapes=[vmem(image, F32)] * 3 + [dma((3,))] * 2, compiler_params=pltpu.CompilerParams(vmem_limit_bytes=56000 * 1024),
    )(*outs)
    return tuple(out[:, None] for out in outs)


def solution(mesh):
    rows_n = mesh.shape["row"]
    groups_n = mesh.shape["slab"] // 2
    ys_n = mesh.shape["coil"] // 2
    tables = transform_tables(rows_n)

    def whole(*args):
        return on_device([jnp.asarray(t) for t in tables], rows_n, groups_n, ys_n, *args)

    image = P(None, "slab", "row", None)
    return jax.shard_map(
        whole,
        mesh=mesh,
        in_specs=(
            image, image, image, P(None, "coil", "slab", "row", None),
            P("row"), P(None, None, "row"), P("row"),
        ),
        out_specs=(image, image, image),
        check_vma=False,
    )
```

time: 78.4 us -> 63.5 us (0.81); the launches traced: 77.4 us -> 63.4 us
  local copies, waits for them, and re-layouts: 9.78 us -> 0 us
  other arithmetic: 3.5 us -> 0 us
  Pallas kernels: 63.5 us -> 62.7 us
    unnamed x19 -> x0, local copies, waits for them, and re-layouts: 9.21 us -> none
    pallas_call x1, Pallas kernels: 63.5 us -> 60.8 us  [on_device(): pl.pallas_call(functools.partial(kernel, rows_n, groups_n, ys_n), out_sha...]
    unnamed x1 -> x0, other arithmetic: 2.13 us -> none
    pallas_call x0 -> x1, Pallas kernels: none -> 1.92 us  [on_device(): pl.pallas_call(put_kernel, out_shape=shapes, in_specs=[far] * 3, out_spec...]
    add x1 -> x0, other arithmetic: 1.37 us -> none  [on_device(): solution_next = solution + step * direction]
where the time goes in v2:
time: 63.5 us; the launch traced here: 63.4 us
  Pallas kernels  62.7 us (99%)
  between operations  0.64 us (1%)
    pallas_call x1, Pallas kernels, on_device(): pl.pallas_call(functools.partial(kernel, rows_n, groups_n, ys_n), out_sha...  60.8 us
    pallas_call x1, Pallas kernels, on_device(): pl.pallas_call(put_kernel, out_shape=shapes, in_specs=[far] * 3, out_spec...  1.92 us

profile of v2, /device:TPU:1, one launch (start us, length us, event | category | flops | bytes accessed | tf_op | source)
XLA Modules:
  0.0 63.4 jit_solution(6853500085316253567)
XLA Ops:
  0.6 60.8 %shard_map.130 = (f32[2,96,384]{2,1,0:T(8,128)}, f32[2,96,384]{2,1,0:T(8,128)}, f32[2,96,384]{2,1,0:T(8,128)}) custom-call(f32[2,96,384]{2,1,0:T(8,128)} %bitcast.20, f32[2,96,384]{2,1,0:T(8,128)} %bitcast.21, f32[2,96,384]{2,1,0:T(8,128)} %bitcast.22, bf16[2,2,96,384]{3,2,1,0:T(8,128)(2,1)} %bitcast.23, s32[4,128]{1,0:T(4,128)} %bitcast.25, ...), custom_call_target="tpu_custom_call" | custom-call | tf_op jit(solution)/shard_map/pallas_call | solution.py:538
  61.5 1.9 %shard_map.131 = (f32[2,96,384]{2,1,0:T(8,128)}, f32[2,96,384]{2,1,0:T(8,128)}, f32[2,96,384]{2,1,0:T(8,128)}) custom-call(f32[2,96,384]{2,1,0:T(8,128)} %get-tuple-element.9.a_ref, f32[2,96,384]{2,1,0:T(8,128)} %get-tuple-element.10.b_ref, f32[2,96,384]{2,1,0:T(8,128)} %get-tuple-element.11.c_ref), custom_call_target="tpu_custom_call" | custom-call | tf_op jit(solution)/shard_map/pallas_call | solution.py:551

commit v3 on v2

--- a/solution.py
+++ b/solution.py
@@ -88,8 +88,8 @@
     fh_ref, fl_ref, bh_ref, bl_ref, in_sem,
     sol_buf, res_buf, dir_buf, out_sem,
     lhs_h, lhs_l, ke_h, ke_l, sinfo, cw, wr, tbuf, yconst, a_h, a_l, s_h, s_l,
-    vsend, vrecv, wall, tz, zrecv, ysum, yrecv, nb, g1, e2, g2, y2,
-    info_s, info_r, val_s, val_r, wt_s, wt_r, g1_s, g1_r, zr_s, zr_r, yr_s, yr_r,
+    vall, wall, scs, tz, zrecv, ysum, yrecv, nb, g1, e2, g2, y2,
+    info_s, info_r, val_s, val_r, sc_s, sc_r, g1_s, g1_r, zr_s, zr_r, yr_s, yr_r,
     e2_s, e2_r, ya_s, ya_r, za_s, za_r, g2_s, g2_r, y2_s, y2_r,
 ):
     slab = lax.axis_index("slab")
@@ -110,8 +110,8 @@
             (sol_in, sol_ref), (bh_in, bh_ref), (bl_in, bl_ref),
         ))
     ]
-    for copy in ins[:9]:
-        copy.start()
+    for i in (0, 1, 7, 2, 3, 4, 5, 6, 8):
+        ins[i].start()
 
     def remote(src, dst, send, recv, slab_to=None, coil_to=None, row_to=None):
         target = (
@@ -174,6 +174,8 @@
     ins[0].wait()
     ins[1].wait()
     sinfo[row, 8 * TAPS : 8 * TAPS + 4] = cell_ref[...].astype(F32)
+    ins[7].wait()
+    sinfo[row, 8 * TAPS + 4 : 8 * TAPS + 8] = dens_ref[...]
 
     pl.semaphore_wait(barrier, count)
     info = [None] + [
@@ -257,6 +259,23 @@
         ke_l[band, 0:192] = low[:, :EXT]
         ke_l[band, 192:384] = low[:, EXT:]
 
+    def lanes(tile):
+        folded = tile[:, 0:128] + tile[:, 128:256] + tile[:, 256:384]
+        return jnp.sum(folded, axis=0, keepdims=True)
+
+    ins[6].wait()
+    dd = lanes(dir_ref[0] * dir_ref[0] + dir_ref[1] * dir_ref[1])
+    rr = lanes(res_ref[0] * res_ref[0] + res_ref[1] * res_ref[1])
+    scs[row, pair] = jnp.concatenate(
+        [dd * (damping / coils), rr * (1.0 / coils), jnp.zeros((6, 128), F32)], axis=0
+    )
+    scc = []
+    for k, e in eight:
+        s, r = eight_to(k, e)
+        scc.append(
+            remote(scs.at[row, pair], scs.at[row, pair], sc_s.at[k, e], sc_r.at[k, e], slab_to=s, row_to=r)
+        )
+
     vals = {}
     for k in orders:
         band = (row + k) % rows_n
@@ -277,50 +296,27 @@
             vr = jnp.sum(vr, axis=0, keepdims=True)
             vi = jnp.sum(vi, axis=0, keepdims=True)
             for b in range(half):
-                vsend[k, c, b : b + 1] = vr[:, 128 * b : 128 * (b + 1)]
-                vsend[k, c, half + b : half + b + 1] = vi[:, 128 * b : 128 * (b + 1)]
-        for e in range(2):
-            if (k, e) == (0, 0):
-                continue
-            c = (pair + e) % 2
-            s, r = eight_to(k, e)
-            vals[k, e] = remote(
-                vsend.at[k, c], vrecv.at[k, e], val_s.at[k, e], val_r.at[k, e], slab_to=s, row_to=r
-            )
-
-    total = vsend[0, pair]
-    for k, e in eight:
-        vals[k, e].wait_recv()
-        total = total + vrecv[k, e]
-    value = 0.5 * total
-    ins[7].wait()
-    dens = dens_ref[...]
-    weighted = value * jnp.concatenate([dens, dens], axis=0)
-    wall[row, pair, 0:8] = weighted
-    curv = jnp.sum(weighted * value, axis=0, keepdims=True) * 2.0
-
-    def lanes(tile):
-        folded = tile[:, 0:128] + tile[:, 128:256] + tile[:, 256:384]
-        return jnp.sum(folded, axis=0, keepdims=True)
-
-    dd = lanes(dir_ref[0] * dir_ref[0] + dir_ref[1] * dir_ref[1])
-    ins[6].wait()
-    rr = lanes(res_ref[0] * res_ref[0] + res_ref[1] * res_ref[1])
-    wall[row, pair, 8:9] = curv + dd * (damping / coils)
-    wall[row, pair, 9:10] = rr * (1.0 / coils)
-    wall[row, pair, 10:16] = jnp.zeros((6, 128), F32)
-    wts = {}
-    for k, e in eight:
-        s, r = eight_to(k, e)
-        wts[k, e] = remote(
-            wall.at[row, pair], wall.at[row, pair], wt_s.at[k, e], wt_r.at[k, e], slab_to=s, row_to=r
-        )
-
+                vall[row, pair, band, c, b : b + 1] = vr[:, 128 * b : 128 * (b + 1)]
+                vall[row, pair, band, c, half + b : half + b + 1] = vi[:, 128 * b : 128 * (b + 1)]
+        for tk, e in eight:
+            s, r = eight_to(tk, e)
+            part = vall.at[row, pair, band]
+            vals[k, tk, e] = remote(part, part, val_s.at[k, tk, e], val_r.at[k, tk, e], slab_to=s, row_to=r)
+
+    power = jnp.zeros((8, 128), F32)
     for k in orders:
         band = (row + k) % rows_n
-        for e in range(2):
-            if (k, e) != (0, 0):
-                wts[(rows_n - k) % rows_n, e].wait_recv()
+        for tk, e in eight:
+            vals[(k + tk) % rows_n, tk, e].wait_recv()
+        total = jnp.zeros((2, 8, 128), F32)
+        for r in range(rows_n):
+            for p in range(2):
+                total = total + vall[r, p, band]
+        value = 0.5 * total
+        dens = sinfo[band, 8 * TAPS + 4 : 8 * TAPS + 8]
+        weighted = value * jnp.concatenate([dens, dens], axis=0)[None]
+        wall[band] = weighted
+        power = power + weighted[0] * value[0] + weighted[1] * value[1]
         for c in range(2):
             w_re = jnp.concatenate([wall[band, c, b : b + 1] for b in range(half)], axis=1)
             w_im = jnp.concatenate([wall[band, c, half + b : half + b + 1] for b in range(half)], axis=1)
@@ -343,10 +339,14 @@
         s_l[band, 0] = low[0:192]
         s_l[band, 1] = low[192:384]
 
+    for copy in scc:
+        copy.wait_recv()
     mine = jnp.zeros((8, 128), F32)
     for r in range(rows_n):
         for c in range(2):
-            mine = mine + wall[r, c, 8:16]
+            mine = mine + scs[r, c]
+    curv = 2.0 * jnp.sum(power, axis=0, keepdims=True)
+    mine = mine + jnp.concatenate([curv, jnp.zeros((7, 128), F32)], axis=0)
 
     def to_across(buf, send, recv):
         copies = []
@@ -521,15 +521,15 @@
         vmem((4, BAND, 128), F32),
         vmem((384, SAMP), BF16), vmem((384, SAMP), BF16),
         vmem((rows_n, 2, 192, EXT), BF16), vmem((rows_n, 2, 192, EXT), BF16),
-        vmem((rows_n, 2, 8, 128), F32), vmem((rows_n, 2, 8, 128), F32),
-        vmem((rows_n, 2, 16, 128), F32),
+        vmem((rows_n, 2, rows_n, 2, 8, 128), F32), vmem((rows_n, 2, 8, 128), F32),
+        vmem((rows_n, 2, 8, 128), F32),
         vmem((BLOCKS, 2, 24, 4, 128), F32), vmem((BLOCKS, 24, 4, 128), F32),
         vmem((ys_n, 40, 128), F32), vmem((ys_n, 40, 128), F32), vmem((2 * ys_n, 40, 128), F32),
         vmem((groups_n, 2, 8, 128), F32), vmem((rows_n, 2, 8, 128), F32),
         vmem((groups_n, 2, 8, 128), F32), vmem((ys_n, 8, 128), F32),
     ]
     few, cross, ys, blocks = (rows_n,), (groups_n, 2), (ys_n,), (BLOCKS,)
-    for shape in (few, eight, eight, cross, blocks, ys, eight, ys, ys, cross, ys):
+    for shape in (few, (rows_n,) + eight, eight, cross, blocks, ys, eight, ys, ys, cross, ys):
         scratch.append(dma(shape))
         scratch.append(dma(shape))
     far = pl.BlockSpec(memory_space=pl.ANY)

time: 63.5 us -> 60.4 us (0.951)
  Pallas kernels: 62.7 us -> 59.7 us
    pallas_call x1, Pallas kernels: 60.8 us -> 57.7 us  [on_device(): pl.pallas_call(functools.partial(kernel, rows_n, groups_n, ys_n), out_sha...]
where the time goes in v3:
time: 60.4 us; the launch traced here: 60.3 us
  Pallas kernels  59.7 us (99%)
  between operations  0.64 us (1%)
    pallas_call x1, Pallas kernels, on_device(): pl.pallas_call(functools.partial(kernel, rows_n, groups_n, ys_n), out_sha...  57.7 us
    pallas_call x1, Pallas kernels, on_device(): pl.pallas_call(put_kernel, out_shape=shapes, in_specs=[far] * 3, out_spec...  1.92 us

profile of v3, /device:TPU:1, one launch (start us, length us, event | category | flops | bytes accessed | tf_op | source)
XLA Modules:
  0.0 60.3 jit_solution(10826931881081470297)
XLA Ops:
  0.6 57.7 %shard_map.130 = (f32[2,96,384]{2,1,0:T(8,128)}, f32[2,96,384]{2,1,0:T(8,128)}, f32[2,96,384]{2,1,0:T(8,128)}) custom-call(f32[2,96,384]{2,1,0:T(8,128)} %bitcast.20, f32[2,96,384]{2,1,0:T(8,128)} %bitcast.21, f32[2,96,384]{2,1,0:T(8,128)} %bitcast.22, bf16[2,2,96,384]{3,2,1,0:T(8,128)(2,1)} %bitcast.23, s32[4,128]{1,0:T(4,128)} %bitcast.25, ...), custom_call_target="tpu_custom_call" | custom-call | tf_op jit(solution)/shard_map/pallas_call | solution.py:538
  58.4 1.9 %shard_map.131 = (f32[2,96,384]{2,1,0:T(8,128)}, f32[2,96,384]{2,1,0:T(8,128)}, f32[2,96,384]{2,1,0:T(8,128)}) custom-call(f32[2,96,384]{2,1,0:T(8,128)} %get-tuple-element.9.a_ref, f32[2,96,384]{2,1,0:T(8,128)} %get-tuple-element.10.b_ref, f32[2,96,384]{2,1,0:T(8,128)} %get-tuple-element.11.c_ref), custom_call_target="tpu_custom_call" | custom-call | tf_op jit(solution)/shard_map/pallas_call | solution.py:551

commit v4 on v3

--- a/solution.py
+++ b/solution.py
@@ -88,9 +88,9 @@
     fh_ref, fl_ref, bh_ref, bl_ref, in_sem,
     sol_buf, res_buf, dir_buf, out_sem,
     lhs_h, lhs_l, ke_h, ke_l, sinfo, cw, wr, tbuf, yconst, a_h, a_l, s_h, s_l,
-    vall, wall, scs, tz, zrecv, ysum, yrecv, nb, g1, e2, g2, y2,
+    vall, wall, scs, tz, zrecv, ysum, yrecv, nb, g1, e2, c2,
     info_s, info_r, val_s, val_r, sc_s, sc_r, g1_s, g1_r, zr_s, zr_r, yr_s, yr_r,
-    e2_s, e2_r, ya_s, ya_r, za_s, za_r, g2_s, g2_r, y2_s, y2_r,
+    e2_s, e2_r, ya_s, ya_r, za_s, za_r, c2_s, c2_r,
 ):
     slab = lax.axis_index("slab")
     coil = lax.axis_index("coil")
@@ -141,9 +141,19 @@
 
     barrier = pltpu.get_barrier_semaphore()
     count = 0
-    for k, e in eight:
-        s, r = eight_to(k, e)
-        pl.semaphore_signal(barrier, inc=1, device_id=(s, coil, r), device_id_type=MESH)
+    slabs = 2 * groups_n
+
+    def hops(d, dr):
+        return min(d, slabs - d) + 4 * min(dr, rows_n - dr)
+
+    wide_set = sorted(
+        ((d, dr) for d in range(slabs) for dr in range(rows_n) if (d, dr) != (0, 0)),
+        key=lambda t: -hops(*t),
+    )
+    for d, dr in wide_set:
+        pl.semaphore_signal(
+            barrier, inc=1, device_id=((slab + d) % slabs, coil, (row + dr) % rows_n), device_id_type=MESH
+        )
         count += 1
     across = [(k, e) for k in range(groups_n) for e in range(2) if (k, e) != (0, 0)]
 
@@ -151,6 +161,8 @@
         return (group + k) % groups_n + groups_n * pair, ((zl + e) % 2) * ys_n + yy
 
     for k, e in across:
+        if k == 0 or e == 0:
+            continue
         s, c = across_to(k, e)
         pl.semaphore_signal(barrier, inc=1, device_id=(s, c, row), device_id_type=MESH)
         count += 1
@@ -158,8 +170,11 @@
     def along_y(k):
         return zl * ys_n + (yy + k) % ys_n
 
-    for k in range(1, ys_n):
-        pl.semaphore_signal(barrier, inc=1, device_id=(slab, along_y(k), row), device_id_type=MESH)
+    coil_set = sorted(range(1, coils), key=lambda k: -min(k % ys_n, ys_n - k % ys_n))
+    for k in coil_set:
+        pl.semaphore_signal(
+            barrier, inc=1, device_id=(slab, (coil + k) % coils, row), device_id_type=MESH
+        )
         count += 1
     near = sorted(range(1, ys_n), key=lambda k: min(k, ys_n - k))
 
@@ -423,14 +438,12 @@
         left = left + gap * gap
     nb[coil, 0:36] = piece[0:36]
     nb[coil, 36:40] = jnp.zeros((4, 128), F32)
-    left = jnp.concatenate([left[0:4] + left[4:8] + left[8:12], jnp.zeros((4, 128), F32)], axis=0)
-    e2[row, pair] = left
-    e2c = []
-    for k, e in eight:
-        s, r = eight_to(k, e)
-        e2c.append(
-            remote(e2.at[row, pair], e2.at[row, pair], e2_s.at[k, e], e2_r.at[k, e], slab_to=s, row_to=r)
-        )
+    e2[slab, row] = jnp.sum(left, axis=0, keepdims=True)
+    e2c = [
+        remote(e2.at[slab, row], e2.at[slab, row], e2_s.at[d, dr], e2_r.at[d, dr],
+               slab_to=(slab + d) % slabs, row_to=(row + dr) % rows_n)
+        for d, dr in wide_set
+    ]
     yac = {
         k: remote(nb.at[coil], nb.at[coil], ya_s.at[k], ya_r.at[k], coil_to=along_y(k)) for k in near
     }
@@ -449,17 +462,18 @@
     outs[0].start()
     for copy in e2c:
         copy.wait_recv()
-    g2[group, zl] = total_of(e2, rows_n, 2)
-    g2c = to_across(g2, g2_s, g2_r)
+    mine = jnp.zeros((1, 128), F32)
+    for i in range(slabs):
+        for r in range(rows_n):
+            mine = mine + e2[i, r]
+    c2[coil] = mine
+    c2c = [
+        remote(c2.at[coil], c2.at[coil], c2_s.at[k], c2_r.at[k], coil_to=(coil + k) % coils)
+        for k in coil_set
+    ]
     for k in near:
         yac[k].wait_recv()
         zac.append(forward(k))
-    for copy in g2c:
-        copy.wait_recv()
-    y2[yy] = total_of(g2, groups_n, 2)
-    y2c = [
-        remote(y2.at[yy], y2.at[yy], y2_s.at[k], y2_r.at[k], coil_to=along_y(k)) for k in range(1, ys_n)
-    ]
     for copy in zac:
         copy.wait_recv()
     for b in range(BLOCKS):
@@ -474,12 +488,11 @@
                 normal = jnp.concatenate(parts, axis=0)
                 res_buf[plane, here, cols] = res_ref[plane, here, cols] - step * normal
     outs[1].start()
-    for copy in y2c:
+    for copy in c2c:
         copy.wait_recv()
-    mine = y2[0]
-    for c in range(1, ys_n):
-        mine = mine + y2[c]
-    folded = jnp.sum(mine[0:4], axis=0, keepdims=True)
+    folded = c2[0]
+    for c in range(1, coils):
+        folded = folded + c2[c]
     ratio = jnp.sum(folded, axis=1, keepdims=True) / norm_now
     dir_buf[...] = res_buf[...] + ratio * dir_ref[...]
     outs[2].start()
@@ -525,11 +538,11 @@
         vmem((rows_n, 2, 8, 128), F32),
         vmem((BLOCKS, 2, 24, 4, 128), F32), vmem((BLOCKS, 24, 4, 128), F32),
         vmem((ys_n, 40, 128), F32), vmem((ys_n, 40, 128), F32), vmem((2 * ys_n, 40, 128), F32),
-        vmem((groups_n, 2, 8, 128), F32), vmem((rows_n, 2, 8, 128), F32),
-        vmem((groups_n, 2, 8, 128), F32), vmem((ys_n, 8, 128), F32),
+        vmem((groups_n, 2, 8, 128), F32),
+        vmem((2 * groups_n, rows_n, 1, 128), F32), vmem((2 * ys_n, 1, 128), F32),
     ]
     few, cross, ys, blocks = (rows_n,), (groups_n, 2), (ys_n,), (BLOCKS,)
-    for shape in (few, (rows_n,) + eight, eight, cross, blocks, ys, eight, ys, ys, cross, ys):
+    for shape in (few, (rows_n,) + eight, eight, cross, blocks, ys, (2 * groups_n, rows_n), ys, ys, (2 * ys_n,)):
         scratch.append(dma(shape))
         scratch.append(dma(shape))
     far = pl.BlockSpec(memory_space=pl.ANY)

time: 60.4 us -> 58.5 us (0.969)
  Pallas kernels: 59.7 us -> 57.8 us
    pallas_call x1, Pallas kernels: 57.7 us -> 55.8 us  [on_device(): pl.pallas_call(functools.partial(kernel, rows_n, groups_n, ys_n), out_sha...]
where the time goes in v4:
time: 58.5 us; the launch traced here: 58.4 us
  Pallas kernels  57.8 us (99%)
  between operations  0.64 us (1%)
    pallas_call x1, Pallas kernels, on_device(): pl.pallas_call(functools.partial(kernel, rows_n, groups_n, ys_n), out_sha...  55.8 us
    pallas_call x1, Pallas kernels, on_device(): pl.pallas_call(put_kernel, out_shape=shapes, in_specs=[far] * 3, out_spec...  1.92 us

profile of v4, /device:TPU:1, one launch (start us, length us, event | category | flops | bytes accessed | tf_op | source)
XLA Modules:
  0.0 58.4 jit_solution(16604129980947130492)
XLA Ops:
  0.6 55.8 %shard_map.130 = (f32[2,96,384]{2,1,0:T(8,128)}, f32[2,96,384]{2,1,0:T(8,128)}, f32[2,96,384]{2,1,0:T(8,128)}) custom-call(f32[2,96,384]{2,1,0:T(8,128)} %bitcast.20, f32[2,96,384]{2,1,0:T(8,128)} %bitcast.21, f32[2,96,384]{2,1,0:T(8,128)} %bitcast.22, bf16[2,2,96,384]{3,2,1,0:T(8,128)(2,1)} %bitcast.23, s32[4,128]{1,0:T(4,128)} %bitcast.25, ...), custom_call_target="tpu_custom_call" | custom-call | tf_op jit(solution)/shard_map/pallas_call | solution.py:551
  56.5 1.9 %shard_map.131 = (f32[2,96,384]{2,1,0:T(8,128)}, f32[2,96,384]{2,1,0:T(8,128)}, f32[2,96,384]{2,1,0:T(8,128)}) custom-call(f32[2,96,384]{2,1,0:T(8,128)} %get-tuple-element.9.a_ref, f32[2,96,384]{2,1,0:T(8,128)} %get-tuple-element.10.b_ref, f32[2,96,384]{2,1,0:T(8,128)} %get-tuple-element.11.c_ref), custom_call_target="tpu_custom_call" | custom-call | tf_op jit(solution)/shard_map/pallas_call | solution.py:564

commit v5 on v4

--- a/solution.py
+++ b/solution.py
@@ -83,10 +83,10 @@
     rows_n, groups_n, ys_n,
     dir_in, res_in, sol_in, sens_in, cell_in, kern_in, dens_in,
     fh_in, fl_in, bh_in, bl_in,
-    sol_out, res_out, dir_out,
+    sol_out, res_out, ratio_out,
     dir_ref, res_ref, sol_ref, sens_ref, cell_ref, dens_ref,
     fh_ref, fl_ref, bh_ref, bl_ref, in_sem,
-    sol_buf, res_buf, dir_buf, out_sem,
+    sol_buf, res_buf, ratio_buf, out_sem,
     lhs_h, lhs_l, ke_h, ke_l, sinfo, cw, wr, tbuf, yconst, a_h, a_l, s_h, s_l,
     vall, wall, scs, tz, zrecv, ysum, yrecv, nb, g1, e2, c2,
     info_s, info_r, val_s, val_r, sc_s, sc_r, g1_s, g1_r, zr_s, zr_r, yr_s, yr_r,
@@ -274,23 +274,6 @@
         ke_l[band, 0:192] = low[:, :EXT]
         ke_l[band, 192:384] = low[:, EXT:]
 
-    def lanes(tile):
-        folded = tile[:, 0:128] + tile[:, 128:256] + tile[:, 256:384]
-        return jnp.sum(folded, axis=0, keepdims=True)
-
-    ins[6].wait()
-    dd = lanes(dir_ref[0] * dir_ref[0] + dir_ref[1] * dir_ref[1])
-    rr = lanes(res_ref[0] * res_ref[0] + res_ref[1] * res_ref[1])
-    scs[row, pair] = jnp.concatenate(
-        [dd * (damping / coils), rr * (1.0 / coils), jnp.zeros((6, 128), F32)], axis=0
-    )
-    scc = []
-    for k, e in eight:
-        s, r = eight_to(k, e)
-        scc.append(
-            remote(scs.at[row, pair], scs.at[row, pair], sc_s.at[k, e], sc_r.at[k, e], slab_to=s, row_to=r)
-        )
-
     vals = {}
     for k in orders:
         band = (row + k) % rows_n
@@ -317,6 +300,23 @@
             s, r = eight_to(tk, e)
             part = vall.at[row, pair, band]
             vals[k, tk, e] = remote(part, part, val_s.at[k, tk, e], val_r.at[k, tk, e], slab_to=s, row_to=r)
+
+    def lanes(tile):
+        folded = tile[:, 0:128] + tile[:, 128:256] + tile[:, 256:384]
+        return jnp.sum(folded, axis=0, keepdims=True)
+
+    ins[6].wait()
+    dd = lanes(dir_ref[0] * dir_ref[0] + dir_ref[1] * dir_ref[1])
+    rr = lanes(res_ref[0] * res_ref[0] + res_ref[1] * res_ref[1])
+    scs[row, pair] = jnp.concatenate(
+        [dd * (damping / coils), rr * (1.0 / coils), jnp.zeros((6, 128), F32)], axis=0
+    )
+    scc = []
+    for k, e in eight:
+        s, r = eight_to(k, e)
+        scc.append(
+            remote(scs.at[row, pair], scs.at[row, pair], sc_s.at[k, e], sc_r.at[k, e], slab_to=s, row_to=r)
+        )
 
     power = jnp.zeros((8, 128), F32)
     for k in orders:
@@ -457,7 +457,7 @@
     sol_buf[...] = sol_ref[...] + step * dir_ref[...]
     outs = [
         pltpu.make_async_copy(src, dst, out_sem.at[i])
-        for i, (src, dst) in enumerate(((sol_buf, sol_out), (res_buf, res_out), (dir_buf, dir_out)))
+        for i, (src, dst) in enumerate(((sol_buf, sol_out), (res_buf, res_out), (ratio_buf, ratio_out)))
     ]
     outs[0].start()
     for copy in e2c:
@@ -494,22 +494,37 @@
     for c in range(1, coils):
         folded = folded + c2[c]
     ratio = jnp.sum(folded, axis=1, keepdims=True) / norm_now
-    dir_buf[...] = res_buf[...] + ratio * dir_ref[...]
+    ratio_buf[...] = jnp.broadcast_to(ratio, (8, 128))
     outs[2].start()
     drain()
     for copy in outs:
         copy.wait()
 
 
-def put_kernel(a_ref, b_ref, c_ref, a_out, b_out, c_out, a_buf, b_buf, c_buf, load_sems, store_sems):
-    refs = ((a_ref, a_buf, a_out), (b_ref, b_buf, b_out), (c_ref, c_buf, c_out))
-    loads = [pltpu.make_async_copy(src, buf, load_sems.at[i]) for i, (src, buf, _) in enumerate(refs)]
-    stores = [pltpu.make_async_copy(buf, dst, store_sems.at[i]) for i, (_, buf, dst) in enumerate(refs)]
+def put_kernel(
+    sol_in, res_in, ratio_in, along_in, sol_out, res_out, dir_out,
+    sol_buf, res_buf, ratio_buf, along_buf, dir_buf, load_sems, store_sems,
+):
+    loads = [
+        pltpu.make_async_copy(src, dst, load_sems.at[i])
+        for i, (src, dst) in enumerate((
+            (res_in, res_buf), (ratio_in, ratio_buf), (along_in, along_buf), (sol_in, sol_buf),
+        ))
+    ]
+    stores = [
+        pltpu.make_async_copy(src, dst, store_sems.at[i])
+        for i, (src, dst) in enumerate(((dir_buf, dir_out), (res_buf, res_out), (sol_buf, sol_out)))
+    ]
     for copy in loads:
         copy.start()
-    for load, store in zip(loads, stores):
-        load.wait()
-        store.start()
+    loads[0].wait()
+    stores[1].start()
+    loads[1].wait()
+    loads[2].wait()
+    dir_buf[...] = res_buf[...] + ratio_buf[0:1, 0:1] * along_buf[...]
+    stores[0].start()
+    loads[3].wait()
+    stores[2].start()
     for copy in stores:
         copy.wait()
 
@@ -524,7 +539,7 @@
         vmem((4, 128), jnp.int32), vmem((4, 128), F32),
         vmem(tables[0].shape, BF16), vmem(tables[1].shape, BF16),
         vmem(tables[2].shape, BF16), vmem(tables[3].shape, BF16), dma((11,)),
-        vmem(image, F32), vmem(image, F32), vmem(image, F32), dma((3,)),
+        vmem(image, F32), vmem(image, F32), vmem((8, 128), F32), dma((3,)),
         vmem((192, 768), BF16), vmem((192, 768), BF16),
         vmem((rows_n, 384, EXT), BF16), vmem((rows_n, 384, EXT), BF16),
         vmem((rows_n, 48, 128), F32),
@@ -550,7 +565,7 @@
     taps = kern.reshape(2, TAPS, 4, 128).transpose(1, 2, 0, 3).reshape(8 * TAPS, 128)
     outs = pl.pallas_call(
         functools.partial(kernel, rows_n, groups_n, ys_n),
-        out_shape=shapes,
+        out_shape=shapes[:2] + (jax.ShapeDtypeStruct((8, 128), F32),),
         in_specs=[far] * 11,
         out_specs=(far,) * 3,
         scratch_shapes=scratch,
@@ -564,10 +579,10 @@
     outs = pl.pallas_call(
         put_kernel,
         out_shape=shapes,
-        in_specs=[far] * 3,
+        in_specs=[far] * 4,
         out_specs=(far,) * 3,
-        scratch_shapes=[vmem(image, F32)] * 3 + [dma((3,))] * 2, compiler_params=pltpu.CompilerParams(vmem_limit_bytes=56000 * 1024),
-    )(*outs)
+        scratch_shapes=[vmem(image, F32)] * 2 + [vmem((8, 128), F32)] + [vmem(image, F32)] * 2 + [dma((4,)), dma((3,))], compiler_params=pltpu.CompilerParams(vmem_limit_bytes=56000 * 1024),
+    )(*outs, direction[:, 0])
     return tuple(out[:, None] for out in outs)
 
 

time: 58.5 us -> 58.2 us (level)
  no operation moved by 1% of the time
where the time goes in v5:
time: 58.2 us; the launch traced here: 58.1 us
  Pallas kernels  57.4 us (99%)
  between operations  0.64 us (1%)
    pallas_call x1, Pallas kernels, on_device(): pl.pallas_call(functools.partial(kernel, rows_n, groups_n, ys_n), out_sha...  55.4 us
    pallas_call x1, Pallas kernels, on_device(): pl.pallas_call(put_kernel, out_shape=shapes, in_specs=[far] * 4, out_spec...  2 us

profile of v5, /device:TPU:1, one launch (start us, length us, event | category | flops | bytes accessed | tf_op | source)
XLA Modules:
  0.0 58.1 jit_solution(10325126198271664456)
XLA Ops:
  0.6 55.4 %shard_map.130 = (f32[2,96,384]{2,1,0:T(8,128)}, f32[2,96,384]{2,1,0:T(8,128)}, f32[8,128]{1,0:T(8,128)}) custom-call(f32[2,96,384]{2,1,0:T(8,128)} %bitcast.20, f32[2,96,384]{2,1,0:T(8,128)} %bitcast.22, f32[2,96,384]{2,1,0:T(8,128)} %bitcast.23, bf16[2,2,96,384]{3,2,1,0:T(8,128)(2,1)} %bitcast.24, s32[4,128]{1,0:T(4,128)} %bitcast.26, f32[40,128]{1,0:T(8,128)} %bitcast.25, ...), custom_call_target="tpu_custom_call" | custom-call | tf_op jit(solution)/shard_map/pallas_call | solution.py:566
  56.1 2.0 %shard_map.131 = (f32[2,96,384]{2,1,0:T(8,128)}, f32[2,96,384]{2,1,0:T(8,128)}, f32[2,96,384]{2,1,0:T(8,128)}) custom-call(f32[2,96,384]{2,1,0:T(8,128)} %get-tuple-element.9.sol_in, f32[2,96,384]{2,1,0:T(8,128)} %get-tuple-element.10.res_in, f32[8,128]{1,0:T(8,128)} %get-tuple-element.11.ratio_in, f32[2,96,384]{2,1,0:T(8,128)} %bitcast.21), custom_call_target="tpu_custom_call" | custom-call | tf_op jit(solution)/shard_map/pallas_call | solution.py:579
